TPU v7x, 512 devices: a whole 4x8x8 slice. The times are simulated.
512 devices in a mesh: leaf: 32 (over x_hi, z, core), tensor: 16 (over y, x_lo).
Axes of the slice: x: 4 (x_hi: 2, x_lo: 2; x = x_hi * 2 + x_lo), y: 8, z: 8, core: 2. Of those that a mesh axis runs over, the one named last changes fastest.
Arguments:
- trunk_kv: bfloat16 [32, 2048, 8, 256], P(None, ('leaf', 'tensor')), may hold values from -6 to 6
- slot_trees: int32 [32], replicated, may hold values from 0 to 31, each once
- trunk_len: int32 [32], replicated, may hold values from 256 to 2048, as said below
- parents: int32 [32, 384], P('leaf'), may hold values from -1 to 382, as said below
- queries: bfloat16 [32, 384, 8192], P('leaf', None, 'tensor'), may hold values from -12 to 12
- branch_kv: bfloat16 [32, 384, 8, 256], P('leaf', 'tensor'), may hold values from -9 to 9
Outputs:
- attended: bfloat16 [32, 384, 8192], P('leaf', None, 'tensor')
Inputs may be any that keep to these rules, and one draw needn't show every extreme that they name: `slot_trees`: each tree is held by exactly one slot. `trunk_len`: every draw has a tree whose length is exactly 2048. parents[s, i] is -1 or one of the 4 tokens just before token i of the same slot; parents[s, 0] is -1.
All inputs are finite; a program needn't handle non-finite values.
Results may differ from a plain program's by a relative error of at most 0.0034.
Values may be sent and summed in bfloat16 or wider, within the bound.
A program may use at most 64 MiB of HBM per device.

v0:
```python
import math

import jax
import jax.numpy as jnp
import numpy as np
from jax import lax
from jax.sharding import PartitionSpec as P

HQ = 64
KVH = 8
HD = 128


key_block = 512
negative_fill = -jnp.inf


def visible_matrices(parent_rows):
    row_count = parent_rows.shape[1]
    places = jnp.arange(row_count, dtype=jnp.int32)
    linked = (parent_rows[:, :, None] == places[None, None, :]) | (
        places[:, None] == places[None, :]
    )[None]
    reached = linked.astype(jnp.bfloat16)
    span = 1
    while span < row_count:
        longer = jnp.einsum("sik,skj->sij", reached, reached, preferred_element_type=jnp.float32)
        reached = (longer > 0.5).astype(jnp.bfloat16)
        span = span * 2
    return reached > 0.5


def spread_heads(values, tensor_count, query_heads, group_size, heads_held):
    head_picks = (
        np.arange(tensor_count)[:, None] * query_heads // group_size
        + np.arange(heads_held)[None, :]
    ).reshape(-1)
    chosen = jnp.take(values, jnp.asarray(head_picks, dtype=jnp.int32), axis=2)
    new_shape = values.shape[:2] + (tensor_count, heads_held) + values.shape[3:]
    return chosen.reshape(new_shape)


def attend_slot(
    query_rows, trunk_side, key_places, length, block_count, branch_side, visible, head_size
):
    row_count = query_rows.shape[0]
    heads_held = trunk_side.shape[1]
    per_head = query_rows.shape[1] // (heads_held * head_size)
    grouped = query_rows.reshape(row_count, heads_held, per_head, head_size)
    score_scale = 1.0 / math.sqrt(head_size)
    branch_scores = (
        jnp.einsum(
            "rkgd,nkd->kgrn",
            grouped,
            branch_side[..., :head_size],
            preferred_element_type=jnp.float32,
        )
        * score_scale
    )
    branch_scores = jnp.where(visible[None, None], branch_scores, negative_fill)
    row_top = jnp.max(branch_scores, axis=-1)
    weights = jnp.exp(branch_scores - row_top[..., None])
    denominator = jnp.sum(weights, axis=-1)
    summed = jnp.einsum(
        "kgrn,nkd->kgrd",
        weights.astype(jnp.bfloat16),
        branch_side[..., head_size:],
        preferred_element_type=jnp.float32,
    )

    def block_step(block_id, running):
        old_top, old_denominator, old_summed = running
        first_key = block_id * key_block
        key_piece = lax.dynamic_slice_in_dim(trunk_side, first_key, key_block, 0)
        places = lax.dynamic_slice_in_dim(key_places, first_key, key_block, 0)
        scores = (
            jnp.einsum(
                "rkgd,nkd->kgrn",
                grouped,
                key_piece[..., :head_size],
                preferred_element_type=jnp.float32,
            )
            * score_scale
        )
        scores = jnp.where((places < length)[None, None, None, :], scores, negative_fill)
        new_top = jnp.maximum(old_top, jnp.max(scores, axis=-1))
        rescale = jnp.exp(old_top - new_top)
        block_weights = jnp.exp(scores - new_top[..., None])
        new_denominator = old_denominator * rescale + jnp.sum(block_weights, axis=-1)
        new_summed = old_summed * rescale[..., None] + jnp.einsum(
            "kgrn,nkd->kgrd",
            block_weights.astype(jnp.bfloat16),
            key_piece[..., head_size:],
            preferred_element_type=jnp.float32,
        )
        return (new_top, new_denominator, new_summed)

    row_top, denominator, summed = lax.fori_loop(
        0, block_count, block_step, (row_top, denominator, summed)
    )
    result = summed / denominator[..., None]
    return result.transpose(2, 0, 1, 3).reshape(row_count, -1).astype(jnp.bfloat16)


def local(trunk_kv, slot_trees, trunk_len, parents, queries, branch_kv):
    tensor_count = lax.axis_size("tensor")
    slot_count, row_count, feature_width = queries.shape
    head_size = HD
    query_heads = feature_width // head_size
    group_size = HQ // KVH
    heads_held = max(1, query_heads // group_size)
    trunk_mid, branch_mine = (
        lax.all_to_all(
            spread_heads(trunk_kv, tensor_count, query_heads, group_size, heads_held),
            "tensor",
            split_axis=2,
            concat_axis=1,
            tiled=True,
        ),
        lax.all_to_all(
            spread_heads(branch_kv, tensor_count, query_heads, group_size, heads_held),
            "tensor",
            split_axis=2,
            concat_axis=1,
            tiled=True,
        ),
    )
    trunk_mid = jnp.take(trunk_mid, slot_trees, axis=0)
    trunk_mine = lax.all_to_all(trunk_mid, "leaf", split_axis=0, concat_axis=1, tiled=True)
    trunk_mine = trunk_mine.reshape(slot_count, -1, heads_held, 2 * head_size)
    branch_mine = branch_mine.reshape(slot_count, row_count, heads_held, 2 * head_size)
    key_total = trunk_mine.shape[1]
    key_ids = jnp.arange(key_total, dtype=jnp.int32)
    all_lengths = jnp.take(trunk_len, slot_trees)
    slot_lengths = lax.dynamic_slice_in_dim(
        all_lengths, lax.axis_index("leaf") * slot_count, slot_count
    )
    block_counts = key_total // key_block
    visible_all = visible_matrices(parents)
    results = [
        attend_slot(
            queries[0],
            trunk_mine[0],
            key_ids,
            slot_lengths[0],
            block_counts,
            branch_mine[0],
            visible_all[0],
            head_size,
        )
    ]
    return jnp.stack(results, axis=0)


def solution(mesh):
    in_specs = (
        P(None, ("leaf", "tensor"), None, None),
        P(),
        P(),
        P("leaf", None),
        P("leaf", None, "tensor"),
        P("leaf", "tensor", None, None),
    )
    out_specs = P("leaf", None, "tensor")
    return jax.shard_map(local, mesh=mesh, in_specs=in_specs, out_specs=out_specs, check_vma=False)
```

profile of v0, /device:TPU:1, one launch (start us, length us, event | category | flops | bytes accessed | tf_op | source)
XLA Modules:
  0.0 128.4 jit_solution(4037255617316502179)
XLA Ops:
  0.0 0.7 pad_clamp_fusion.1
  0.7 0.3 copy-done
  1.1 3.5 %gather_fusion.2 = bf16[16,32,4,256]{3,0,2,1:T(8,128)(2,1)S(1)} fusion(bf16[32,4,8,256]{3,2,1,0:T(8,128)(2,1)S(1)} %copy-done, s32[1024]{0:T(1024)S(1)} %pad_clamp_fusion.1), kind=kCustom, calls=%fused_computation.2 | custom fusion | bytes 2097216 | tf_op jit(solution)/shard_map/jit(_take)/gather | solution.py:38
  4.6 1.5 %copy.40 = bf16[32,4,16,1,256]{4,1,0,3,2:T(4,128)(2,1)} copy(bf16[32,4,16,1,256]{4,2,1,0,3:T(8,128)(2,1)S(1)} %bitcast.171) | data formatting | bytes 2097152 | tf_op jit(solution)/shard_map/jit(_take)/gather | solution.py:38
  6.2 8.7 %all-to-all-start.1 = ((bf16[32,4,16,1,256]{4,1,0,3,2:T(4,128)(2,1)}), bf16[32,4,16,1,256]{4,1,0,3,2:T(4,128)(2,1)S(1)}, u32[]{:S(2)}, u32[]{:S(2)}) async-start(bf16[32,4,16,1,256]{4,1,0,3,2:T(4,128)(2,1)} %copy.40), calls=%async_computation.1 | async-start | bytes 2097152 | tf_op jit(solution)/shard_map/all_to_all | solution.py:113
  14.9 1.2 gather_fusion
  16.1 0.7 gather_fusion.1
  16.8 22.5 %all-to-all-done.1 = bf16[32,4,16,1,256]{4,1,0,3,2:T(4,128)(2,1)S(1)} async-done(((bf16[32,4,16,1,256]{4,1,0,3,2:T(4,128)(2,1)}), bf16[32,4,16,1,256]{4,1,0,3,2:T(4,128)(2,1)S(1)}, u32[]{:S(2)}, u32[]{:S(2)}) %all-to-all-start.1) | async-done | bytes 1048608 | tf_op jit(solution)/shard_map/all_to_all | solution.py:113
  39.3 7.2 %all-to-all-start = ((bf16[1,24,16,1,256]{4,1,3,0,2:T(8,128)(2,1)}), bf16[1,24,16,1,256]{4,1,3,0,2:T(8,128)(2,1)S(1)}, u32[]{:S(2)}, u32[]{:S(2)}) async-start(bf16[1,24,16,1,256]{4,1,3,0,2:T(8,128)(2,1)} %bitcast.17), calls=%async_computation | async-start | bytes 393216 | tf_op jit(solution)/shard_map/all_to_all | solution.py:120
  46.5 0.2 copy.41
  46.7 0.6 copy.42
  47.3 0.6 gather_fusion.3
  48.0 1.1 fusion.34
  49.1 6.6 %all-to-all-done = bf16[1,24,16,1,256]{4,1,3,0,2:T(8,128)(2,1)S(1)} async-done(((bf16[1,24,16,1,256]{4,1,3,0,2:T(8,128)(2,1)}), bf16[1,24,16,1,256]{4,1,3,0,2:T(8,128)(2,1)S(1)}, u32[]{:S(2)}, u32[]{:S(2)}) %all-to-all-start) | async-done | bytes 196640 | tf_op jit(solution)/shard_map/all_to_all | solution.py:120
  55.7 15.3 %all-to-all-start.2 = ((bf16[32,64,1,1,256]{4,1,3,2,0:T(8,128)(2,1)}), bf16[32,64,1,1,256]{4,1,3,2,0:T(8,128)(2,1)S(1)}, u32[]{:S(2)}, u32[]{:S(2)}) async-start(bf16[32,64,1,1,256]{4,1,3,2,0:T(8,128)(2,1)} %fusion.34), calls=%async_computation.2 | async-start | bytes 2097152 | tf_op jit(solution)/shard_map/all_to_all | solution.py:129
  71.1 0.2 copy.44
  71.4 0.5 convolution_compare_fusion.8
  71.9 0.9 convolution_compare_fusion.6
  72.7 0.9 convolution_compare_fusion.4
  73.6 0.9 convolution_compare_fusion.2
  74.4 0.9 fusion.33
  75.3 0.3 copy.35
  75.6 0.2 copy.45
  75.8 0.6 dynamic_slice.17
  76.4 0.5 fusion.25
  76.9 0.5 fusion.24
  77.4 0.7 convolution_bitcast_fusion
  78.2 20.6 %all-to-all-done.2 = bf16[32,64,1,1,256]{4,1,3,2,0:T(8,128)(2,1)S(1)} async-done(((bf16[32,64,1,1,256]{4,1,3,2,0:T(8,128)(2,1)}), bf16[32,64,1,1,256]{4,1,3,2,0:T(8,128)(2,1)S(1)}, u32[]{:S(2)}, u32[]{:S(2)}) %all-to-all-start.2) | async-done | bytes 1048608 | tf_op jit(solution)/shard_map/all_to_all | solution.py:129
  98.7 28.1 %while.17 = (s32[]{:T(128)}, f32[1,4,384]{2,1,0:T(4,128)S(1)}, f32[1,4,384]{2,1,0:T(4,128)S(1)}, f32[1,4,384,128]{3,2,1,0:T(8,128)S(1)}, s32[2048]{0:T(1024)S(1)...) while((s32[]{:T(128)}, f32[1,4,384]{2,1,0:T(4,128)S(1)}, ...), condition=%wide.region_5.6_spmd, body=%wide.region_2.5_spmd.sunk | while | flops 411702272 | bytes 24350952 | solution.py:98
  98.7 0.6 dynamic-slice_compare_fusion.2
  99.4 2.2 %bitcast_reduce_fusion.2 = (f32[4,384]{1,0:T(4,128)S(1)}, f32[512,384,4]{1,0,2:T(8,128)}) fusion(pred[512]{0:T(512)(128)(4,1)S(1)} %dynamic-slice_compare_fusion.2, bf16[384,1,4,128]{3,0,2,1:T(8,128)(2,1)S(1)} %get-tuple-element.285, bf16[2048,1,256]{2,0,1:T(8,128)(2,1)S(1)} %get-tuple-element.284, s32[]{:T(128)S(6)} %select_n.132), kind=kOutput, calls=%fused_computation.5.clone.1 | convolution fusion | flops 203684352 | bytes 3676676 | tf_op jit(solution)/shard_map/while/body/eval_jaxpr/rkgd,nkd->kgrn/dot_general | solution.py:77
  101.6 3.4 %fusion.67 = f32[1,4,384,128]{3,2,1,0:T(8,128)S(1)} fusion(f32[512,384,4]{1,0,2:T(8,128)} %get-tuple-element.250, f32[4,384]{1,0:T(4,128)S(1)} %bitcast.174, pred[512]{0:T(512)(128)(4,1)S(1)} %dynamic-slice_compare_fusion.2, f32[1,4,384,128]{3,2,1,0:T(8,128)S(1)} %get-tuple-element.268, f32[4,384]{1,0:T(4,128)S(1)} %get-tuple-element.251, ...), kind=kOutput, calls=%fused_computation.17.clone.1 | convolution fusion | flops 204865536 | bytes 4862472 | tf_op jit(solution)/shard_map/while/body/eval_jaxpr/kgrn,nkd->kgrd/dot_general | solution.py:90
  105.0 0.7 fusion.66
  105.8 0.6 dynamic-slice_compare_fusion.2
  106.4 2.2 %bitcast_reduce_fusion.2 = (f32[4,384]{1,0:T(4,128)S(1)}, f32[512,384,4]{1,0,2:T(8,128)}) fusion(pred[512]{0:T(512)(128)(4,1)S(1)} %dynamic-slice_compare_fusion.2, bf16[384,1,4,128]{3,0,2,1:T(8,128)(2,1)S(1)} %get-tuple-element.285, bf16[2048,1,256]{2,0,1:T(8,128)(2,1)S(1)} %get-tuple-element.284, s32[]{:T(128)S(6)} %select_n.132), kind=kOutput, calls=%fused_computation.5.clone.1 | convolution fusion | flops 203684352 | bytes 3676676 | tf_op jit(solution)/shard_map/while/body/eval_jaxpr/rkgd,nkd->kgrn/dot_general | solution.py:77
  108.6 3.4 %fusion.67 = f32[1,4,384,128]{3,2,1,0:T(8,128)S(1)} fusion(f32[512,384,4]{1,0,2:T(8,128)} %get-tuple-element.250, f32[4,384]{1,0:T(4,128)S(1)} %bitcast.174, pred[512]{0:T(512)(128)(4,1)S(1)} %dynamic-slice_compare_fusion.2, f32[1,4,384,128]{3,2,1,0:T(8,128)S(1)} %get-tuple-element.268, f32[4,384]{1,0:T(4,128)S(1)} %get-tuple-element.251, ...), kind=kOutput, calls=%fused_computation.17.clone.1 | convolution fusion | flops 204865536 | bytes 4862472 | tf_op jit(solution)/shard_map/while/body/eval_jaxpr/kgrn,nkd->kgrd/dot_general | solution.py:90
  112.0 0.7 fusion.66
  112.8 0.6 dynamic-slice_compare_fusion.2
  113.4 2.2 %bitcast_reduce_fusion.2 = (f32[4,384]{1,0:T(4,128)S(1)}, f32[512,384,4]{1,0,2:T(8,128)}) fusion(pred[512]{0:T(512)(128)(4,1)S(1)} %dynamic-slice_compare_fusion.2, bf16[384,1,4,128]{3,0,2,1:T(8,128)(2,1)S(1)} %get-tuple-element.285, bf16[2048,1,256]{2,0,1:T(8,128)(2,1)S(1)} %get-tuple-element.284, s32[]{:T(128)S(6)} %select_n.132), kind=kOutput, calls=%fused_computation.5.clone.1 | convolution fusion | flops 203684352 | bytes 3676676 | tf_op jit(solution)/shard_map/while/body/eval_jaxpr/rkgd,nkd->kgrn/dot_general | solution.py:77
  115.7 3.4 %fusion.67 = f32[1,4,384,128]{3,2,1,0:T(8,128)S(1)} fusion(f32[512,384,4]{1,0,2:T(8,128)} %get-tuple-element.250, f32[4,384]{1,0:T(4,128)S(1)} %bitcast.174, pred[512]{0:T(512)(128)(4,1)S(1)} %dynamic-slice_compare_fusion.2, f32[1,4,384,128]{3,2,1,0:T(8,128)S(1)} %get-tuple-element.268, f32[4,384]{1,0:T(4,128)S(1)} %get-tuple-element.251, ...), kind=kOutput, calls=%fused_computation.17.clone.1 | convolution fusion | flops 204865536 | bytes 4862472 | tf_op jit(solution)/shard_map/while/body/eval_jaxpr/kgrn,nkd->kgrd/dot_general | solution.py:90
  119.1 0.7 fusion.66
  119.9 0.6 dynamic-slice_compare_fusion.2
  120.5 2.2 %bitcast_reduce_fusion.2 = (f32[4,384]{1,0:T(4,128)S(1)}, f32[512,384,4]{1,0,2:T(8,128)}) fusion(pred[512]{0:T(512)(128)(4,1)S(1)} %dynamic-slice_compare_fusion.2, bf16[384,1,4,128]{3,0,2,1:T(8,128)(2,1)S(1)} %get-tuple-element.285, bf16[2048,1,256]{2,0,1:T(8,128)(2,1)S(1)} %get-tuple-element.284, s32[]{:T(128)S(6)} %select_n.132), kind=kOutput, calls=%fused_computation.5.clone.1 | convolution fusion | flops 203684352 | bytes 3676676 | tf_op jit(solution)/shard_map/while/body/eval_jaxpr/rkgd,nkd->kgrn/dot_general | solution.py:77
  122.7 3.4 %fusion.67 = f32[1,4,384,128]{3,2,1,0:T(8,128)S(1)} fusion(f32[512,384,4]{1,0,2:T(8,128)} %get-tuple-element.250, f32[4,384]{1,0:T(4,128)S(1)} %bitcast.174, pred[512]{0:T(512)(128)(4,1)S(1)} %dynamic-slice_compare_fusion.2, f32[1,4,384,128]{3,2,1,0:T(8,128)S(1)} %get-tuple-element.268, f32[4,384]{1,0:T(4,128)S(1)} %get-tuple-element.251, ...), kind=kOutput, calls=%fused_computation.17.clone.1 | convolution fusion | flops 204865536 | bytes 4862472 | tf_op jit(solution)/shard_map/while/body/eval_jaxpr/kgrn,nkd->kgrd/dot_general | solution.py:90
  126.1 0.7 fusion.66
  126.9 0.3 fusion.40
  127.2 0.3 copy.46
  127.5 0.9 convert_element_type.43
  (38 shorter events, 0.3 us)
Async XLA Ops:
  0.0 1.1 copy-start
  4.6 10.2 %copy-start.4 = (bf16[1,24,8,256]{3,2,1,0:T(8,128)(2,1)S(1)}, bf16[1,24,8,256]{3,2,1,0:T(8,128)(2,1)}, u32[]{:S(2)}) copy-start(bf16[1,24,8,256]{3,2,1,0:T(8,128)(2,1)} %param.15) | copy-start | bytes 294916
  4.6 11.5 %copy-start.6 = (s32[32]{0:T(128)S(1)}, s32[32]{0:T(128)}, u32[]{:S(2)}) copy-start(s32[32]{0:T(128)} %param.11) | copy-start | bytes 388
  4.6 11.5 %copy-start.1 = (s32[32]{0:T(128)S(1)}, s32[32]{0:T(128)}, u32[]{:S(2)}) copy-start(s32[32]{0:T(128)} %param.12) | copy-start | bytes 388
  6.2 33.2 %all-to-all-start.1 = ((bf16[32,4,16,1,256]{4,1,0,3,2:T(4,128)(2,1)}), bf16[32,4,16,1,256]{4,1,0,3,2:T(4,128)(2,1)S(1)}, u32[]{:S(2)}, u32[]{:S(2)}) async-start(bf16[32,4,16,1,256]{4,1,0,3,2:T(4,128)(2,1)} %copy.40), calls=%async_computation.1 | async-start | bytes 2097152 | tf_op jit(solution)/shard_map/all_to_all | solution.py:113
  39.3 16.3 %all-to-all-start = ((bf16[1,24,16,1,256]{4,1,3,0,2:T(8,128)(2,1)}), bf16[1,24,16,1,256]{4,1,3,0,2:T(8,128)(2,1)S(1)}, u32[]{:S(2)}, u32[]{:S(2)}) async-start(bf16[1,24,16,1,256]{4,1,3,0,2:T(8,128)(2,1)} %bitcast.17), calls=%async_computation | async-start | bytes 393216 | tf_op jit(solution)/shard_map/all_to_all | solution.py:120
  47.9 23.1 %copy-start.3 = (bf16[1,384,512]{2,1,0:T(8,128)(2,1)S(1)}, bf16[1,384,512]{2,1,0:T(8,128)(2,1)}, u32[]{:S(2)}) copy-start(bf16[1,384,512]{2,1,0:T(8,128)(2,1)} %param.14) | copy-start | bytes 1179652
  49.1 22.2 %copy-start.5 = (s32[1,384]{1,0:T(1,128)S(1)}, s32[1,384]{1,0:T(1,128)}, u32[]{:S(2)}) copy-start(s32[1,384]{1,0:T(1,128)} %param.13) | copy-start | bytes 4612
  55.7 43.1 %all-to-all-start.2 = ((bf16[32,64,1,1,256]{4,1,3,2,0:T(8,128)(2,1)}), bf16[32,64,1,1,256]{4,1,3,2,0:T(8,128)(2,1)S(1)}, u32[]{:S(2)}, u32[]{:S(2)}) async-start(bf16[32,64,1,1,256]{4,1,3,2,0:T(8,128)(2,1)} %fusion.34), calls=%async_computation.2 | async-start | bytes 2097152 | tf_op jit(solution)/shard_map/all_to_all | solution.py:129
  101.6 3.4 %copy-start.2 = (f32[512,384,4]{1,0,2:T(8,128)S(1)}, f32[512,384,4]{1,0,2:T(8,128)}, u32[]{:S(2)}) copy-start(f32[512,384,4]{1,0,2:T(8,128)} %get-tuple-element.250) | copy-start | bytes 9437188 | tf_op jit(solution)/shard_map/while
  108.6 3.4 %copy-start.2 = (f32[512,384,4]{1,0,2:T(8,128)S(1)}, f32[512,384,4]{1,0,2:T(8,128)}, u32[]{:S(2)}) copy-start(f32[512,384,4]{1,0,2:T(8,128)} %get-tuple-element.250) | copy-start | bytes 9437188 | tf_op jit(solution)/shard_map/while
  115.7 3.4 %copy-start.2 = (f32[512,384,4]{1,0,2:T(8,128)S(1)}, f32[512,384,4]{1,0,2:T(8,128)}, u32[]{:S(2)}) copy-start(f32[512,384,4]{1,0,2:T(8,128)} %get-tuple-element.250) | copy-start | bytes 9437188 | tf_op jit(solution)/shard_map/while
  122.7 3.4 %copy-start.2 = (f32[512,384,4]{1,0,2:T(8,128)S(1)}, f32[512,384,4]{1,0,2:T(8,128)}, u32[]{:S(2)}) copy-start(f32[512,384,4]{1,0,2:T(8,128)} %get-tuple-element.250) | copy-start | bytes 9437188 | tf_op jit(solution)/shard_map/while
where the time goes:
time: 130 us; the launch traced here: 128 us
  waiting for transfers between devices  49.6 us (38%)
  starting transfers between devices  31.2 us (24%)
  matrix products  27.6 us (21%)
  local copies, waits for them, and re-layouts  11.4 us (9%)
  other arithmetic  8.15 us (6%)
    all_to_all x1, waiting for transfers between devices, local(): lax.all_to_all(spread_heads(trunk_kv, tensor_count, query_heads, group_si...  22.5 us
    all_to_all x1, waiting for transfers between devices, local(): lax.all_to_all(trunk_mid, 'leaf', split_axis=0, concat_axis=1, tiled=True)  20.6 us
    all_to_all x1, starting transfers between devices, local(): lax.all_to_all(trunk_mid, 'leaf', split_axis=0, concat_axis=1, tiled=True)  15.3 us
    dot_general x4, matrix products, block_step(): jnp.einsum('kgrn,nkd->kgrd', block_weights.astype(jnp.bfloat16), key_piec...  13.6 us
    dot_general x4, matrix products, block_step(): jnp.einsum('rkgd,nkd->kgrn', grouped, key_piece[..., :head_size], preferr...  8.89 us
    all_to_all x1, starting transfers between devices, local(): lax.all_to_all(spread_heads(trunk_kv, tensor_count, query_heads, group_si...  8.68 us
    all_to_all x1, starting transfers between devices, local(): lax.all_to_all(spread_heads(branch_kv, tensor_count, query_heads, group_s...  7.19 us
    all_to_all x1, waiting for transfers between devices, local(): lax.all_to_all(spread_heads(branch_kv, tensor_count, query_heads, group_s...  6.56 us
  transfers between devices with their start and end apart: 3, of which 3 were waited for; matrix products, arithmetic and copies ran while one was open for 9% of the time, Pallas kernels for 0%

commit v1 on v0

v1 whole, which is shorter than its diff:
```python
import math

import jax
import jax.numpy as jnp
import numpy as np
from jax import lax
from jax.experimental import pallas as pl
from jax.experimental.pallas import tpu as pltpu
from jax.sharding import PartitionSpec as P

MESH = pl.DeviceIdType.MESH

HQ = 64
KVH = 8
HD = 128
BR = 384
TREES = 32
HEADS = 4
NZ = 8
NY = 8
CHUNKS = 4
DEAD = -1e30
SCORE_SCALE = math.log2(math.e) / math.sqrt(HD)

def head_order():
    picks = np.zeros((128, 128), np.float32)
    for head in range(8):
        for target in range(4):
            for pos in range(4):
                picks[head * 16 + target * 4 + pos, target * 32 + pos * 8 + head] = 1
    return picks


def target_order():
    picks = np.zeros((256, 256), np.float32)
    for source in range(16):
        for target in range(4):
            for pos in range(4):
                picks[target * 64 + source * 4 + pos, source * 16 + target * 4 + pos] = 1
    return picks


def branch_out_order():
    picks = np.zeros((384, 384), np.float32)
    for head in range(8):
        for half in range(2):
            for token in range(24):
                picks[head * 48 + half * 24 + token, half * 192 + token * 8 + head] = 1
    return picks


def branch_in_order():
    picks = np.zeros((2, 96, 96), np.float32)
    for x_lo in range(2):
        for half in range(2):
            for source in range(2):
                for token in range(24):
                    other = (source + x_lo) % 2
                    picks[x_lo, half * 48 + source * 24 + token, other * 48 + half * 24 + token] = 1
    return picks


def kernel(
    slots, lengths, trunk, branch, queries, parents, pick_head, pick_target, pick_out, pick_in,
    out,
    staged, landed, sorted_rows, keys_values, branch_staged, branch_landed, branch_kv,
    turned, shown, top, total, summed,
    send_a, recv_a, send_b, recv_b, send_r, recv_r, send_p, recv_p,
):
    leaf = lax.axis_index("leaf")
    tensor = lax.axis_index("tensor")
    xh, z, c = leaf // 16, (leaf // 2) % 8, leaf % 2
    y, xl = tensor // 2, tensor % 2

    def place(xh, z, c, y, xl):
        return ((xh * 8 + z) * 2 + c, y * 2 + xl)

    barrier = pltpu.get_barrier_semaphore()

    def greet_plane(step, _):
        pl.semaphore_signal(
            barrier, inc=1, device_id=place(xh, (z + step // 8) % 8, c, (y + step % 8) % 8, xl),
            device_id_type=MESH,
        )
        return 0

    lax.fori_loop(1, NZ * NY, greet_plane, 0)

    def ring_place(step):
        return place((xh + step // 4) % 2, z, (c + (step // 2) % 2) % 2, y, (xl + step % 2) % 2)

    for step in range(1, 8):
        pl.semaphore_signal(barrier, inc=1, device_id=ring_place(step), device_id_type=MESH)

    def offset_of(group):
        return jnp.where(group % 2 == 0, (group // 2 + 1) % 4, 7 - group // 2)

    def stage(group):
        z_to = (z + offset_of(group)) % 8
        rows = jnp.concatenate(
            [trunk[slots[((q // 2) * 8 + z_to) * 2 + q % 2]] for q in range(4)], axis=0
        )
        ordered = jnp.dot(pick_head[...], rows, preferred_element_type=jnp.float32)
        ordered = ordered.astype(jnp.bfloat16)
        for head in range(8):
            staged[group, head] = ordered[head * 16 : head * 16 + 16]

    def send_plane(group):
        z_to = (z + offset_of(group)) % 8
        for dy in (4, 3, 5, 2, 6, 1, 7, 0):
            y_to = (y + dy) % 8

            def send():
                pltpu.make_async_remote_copy(
                    src_ref=staged.at[group, y_to],
                    dst_ref=landed.at[group * 8 + dy],
                    send_sem=send_a,
                    recv_sem=recv_a.at[group // 2],
                    device_id=place(xh, z_to, c, y_to, xl),
                    device_id_type=MESH,
                ).start()

            if dy == 0:
                pl.when(group != 6)(send)
            else:
                send()

    def stage_and_send(group, _):
        stage(group)
        send_plane(group)
        return 0

    pl.semaphore_wait(barrier, NZ * NY - 1 + 7)
    lax.fori_loop(0, 4, stage_and_send, 0)

    rows = jnp.concatenate([branch[:, :HD], branch[:, HD:]], axis=0)
    ordered = jnp.dot(pick_out[...], rows, preferred_element_type=jnp.float32).astype(jnp.bfloat16)
    for head in range(8):
        branch_staged[head] = ordered[head * 48 : head * 48 + 48]
    for dy in (4, 3, 5, 2, 6, 1, 7):
        y_to = (y + dy) % 8
        pltpu.make_async_remote_copy(
            src_ref=branch_staged.at[y_to],
            dst_ref=branch_landed.at[0, dy],
            send_sem=send_r,
            recv_sem=recv_r,
            device_id=place(xh, z, c, y_to, xl),
            device_id_type=MESH,
        ).start()
    branch_landed[0, 0] = branch_staged[y]

    lax.fori_loop(4, 8, stage_and_send, 0)
    landed[48] = staged[6, y]

    above = lax.broadcasted_iota(jnp.int32, (BR, BR), 0)
    along = lax.broadcasted_iota(jnp.int32, (BR, BR), 1)
    linked = jnp.logical_or(above == parents[...], above == along)
    shown[...] = jnp.where(linked, 1.0, 0.0).astype(jnp.bfloat16)

    def lengthen(_, carry):
        reached = shown[...]
        longer = jnp.dot(reached, reached, preferred_element_type=jnp.float32)
        shown[...] = jnp.where(longer > 0.5, 1.0, 0.0).astype(jnp.bfloat16)
        return carry

    lax.fori_loop(0, 9, lengthen, 0)

    for head in range(HEADS):
        turned[head] = jnp.transpose(queries[:, head * HD : head * HD + HD])

    def wait_bytes(ref, sem):
        pltpu.make_async_copy(ref, ref, sem).wait()

    def pass_on(chunk):
        if chunk < 3:
            wait_bytes(landed.at[chunk * 16 : chunk * 16 + 16], recv_a.at[chunk])
        else:
            wait_bytes(landed.at[49:64], recv_a.at[chunk])
        rows = landed[chunk * 16 : chunk * 16 + 16].reshape(256, 256)
        ordered = jnp.dot(pick_target[...], rows, preferred_element_type=jnp.float32)
        ordered = ordered.astype(jnp.bfloat16)
        for target in range(4):
            sorted_rows[chunk, target] = ordered[target * 64 : target * 64 + 64]
        for step in (5, 7, 4, 6, 1, 3, 2):
            target = ((xh + step // 4) % 2) * 2 + (c + (step // 2) % 2) % 2
            pltpu.make_async_remote_copy(
                src_ref=sorted_rows.at[chunk, target],
                dst_ref=keys_values.at[chunk, step],
                send_sem=send_b,
                recv_sem=recv_b.at[chunk],
                device_id=ring_place(step),
                device_id_type=MESH,
            ).start()
        keys_values[chunk, 0] = sorted_rows[chunk, xh * 2 + c]

    def attend(keys, values, mask, first):
        def one_head(head, _):
            scores = jnp.dot(keys, turned[head], preferred_element_type=jnp.float32)
            scores = scores * SCORE_SCALE + mask
            best = jnp.max(scores, axis=0, keepdims=True)
            if not first:
                best = jnp.maximum(best, top[head])
            weights = jnp.exp2(scores - best)
            weight_sum = jnp.sum(weights, axis=0, keepdims=True)
            product = lax.dot_general(
                values, weights.astype(jnp.bfloat16), (((0,), (0,)), ((), ())),
                preferred_element_type=jnp.float32,
            )
            if first:
                total[head] = weight_sum
                summed[head] = product
            else:
                fade = jnp.exp2(top[head] - best)
                total[head] = total[head] * fade + weight_sum
                summed[head] = summed[head] * fade + product
            top[head] = best
            return 0

        lax.fori_loop(0, HEADS, one_head, 0)

    length = lengths[slots[leaf]]

    def attend_chunk(chunk):
        wait_bytes(keys_values.at[chunk, 1:8], recv_b.at[chunk])
        both = keys_values[chunk].reshape(512, 256)
        key = lax.broadcasted_iota(jnp.int32, (512, 1), 0)
        source = key >> 6
        xh_from = (xh + (source >> 2)) & 1
        c_from = (c + ((source >> 1) & 1)) & 1
        xl_from = (xl + (source & 1)) & 1
        dz = jnp.where(((key >> 5) & 1) == 0, (chunk + 1) % 4, 7 - chunk)
        z_from = (z - dz + 8) & 7
        y_from = (y - ((key >> 2) & 7) + 8) & 7
        position = (((xh_from * 8 + z_from) * 2 + c_from) * 16 + y_from * 2 + xl_from) * 4 + (key & 3)
        mask = jnp.where(position < length, 0.0, DEAD)
        attend(both[:, :HD], both[:, HD:], mask, False)

    def attend_branch():
        wait_bytes(branch_landed.at[1], recv_p)
        order = pick_in[xl]
        for dy in range(8):
            y_from = (y - dy + 8) % 8
            rows = jnp.concatenate([branch_landed[0, dy], branch_landed[1, dy]], axis=0)
            ordered = jnp.dot(order, rows, preferred_element_type=jnp.float32).astype(jnp.bfloat16)
            branch_kv[0, y_from] = ordered[:48]
            branch_kv[1, y_from] = ordered[48:]
        mask = jnp.where(shown[...] > 0.5, 0.0, DEAD)
        attend(branch_kv[0].reshape(BR, HD), branch_kv[1].reshape(BR, HD), mask, True)

    pass_on(0)
    pass_on(1)
    wait_bytes(branch_landed.at[0, 1:8], recv_r)
    pltpu.make_async_remote_copy(
        src_ref=branch_landed.at[0],
        dst_ref=branch_landed.at[1],
        send_sem=send_p,
        recv_sem=recv_p,
        device_id=ring_place(1),
        device_id_type=MESH,
    ).start()
    pass_on(2)
    attend_branch()
    attend_chunk(0)
    pass_on(3)
    attend_chunk(1)
    attend_chunk(2)
    attend_chunk(3)

    for head in range(HEADS):
        result = summed[head] / total[head]
        out[:, head * HD : head * HD + HD] = jnp.transpose(result).astype(jnp.bfloat16)

    wait_bytes(landed.at[1:64], send_a)
    wait_bytes(branch_landed.at[0, 1:8], send_r)
    wait_bytes(branch_landed.at[0], send_p)
    wait_bytes(keys_values.at[:, 1:8], send_b)


def local(trunk_kv, slot_trees, trunk_len, parents, queries, branch_kv):
    vmem = pl.BlockSpec(memory_space=pltpu.VMEM)
    smem = pl.BlockSpec(memory_space=pltpu.SMEM)
    picks = [
        jnp.asarray(table(), dtype=jnp.bfloat16)
        for table in (head_order, target_order, branch_out_order, branch_in_order)
    ]
    attended = pl.pallas_call(
        kernel,
        out_shape=jax.ShapeDtypeStruct((BR, HEADS * HD), jnp.bfloat16),
        in_specs=[smem, smem] + [vmem] * 8,
        out_specs=vmem,
        scratch_shapes=[
            pltpu.VMEM((8, 8, 16, 256), jnp.bfloat16),
            pltpu.VMEM((64, 16, 256), jnp.bfloat16),
            pltpu.VMEM((CHUNKS, 4, 64, 256), jnp.bfloat16),
            pltpu.VMEM((CHUNKS, 8, 64, 256), jnp.bfloat16),
            pltpu.VMEM((8, 48, HD), jnp.bfloat16),
            pltpu.VMEM((2, 8, 48, HD), jnp.bfloat16),
            pltpu.VMEM((2, 8, 48, HD), jnp.bfloat16),
            pltpu.VMEM((HEADS, HD, BR), jnp.bfloat16),
            pltpu.VMEM((BR, BR), jnp.bfloat16),
            pltpu.VMEM((HEADS, 1, BR), jnp.float32),
            pltpu.VMEM((HEADS, 1, BR), jnp.float32),
            pltpu.VMEM((HEADS, HD, BR), jnp.float32),
            pltpu.SemaphoreType.DMA,
            pltpu.SemaphoreType.DMA((CHUNKS,)),
            pltpu.SemaphoreType.DMA,
            pltpu.SemaphoreType.DMA((CHUNKS,)),
            pltpu.SemaphoreType.DMA,
            pltpu.SemaphoreType.DMA,
            pltpu.SemaphoreType.DMA,
            pltpu.SemaphoreType.DMA,
        ],
        compiler_params=pltpu.CompilerParams(
            collective_id=0, has_side_effects=True, vmem_limit_bytes=40 * 1024 * 1024
        ),
    )(
        slot_trees,
        trunk_len,
        trunk_kv.reshape(TREES, 32, 2 * HD),
        branch_kv.reshape(192, 2 * HD),
        queries.reshape(BR, HEADS * HD),
        parents,
        *picks,
    )
    return attended.reshape(1, BR, HEADS * HD)


def solution(mesh):
    in_specs = (
        P(None, ("leaf", "tensor"), None, None),
        P(),
        P(),
        P("leaf", None),
        P("leaf", None, "tensor"),
        P("leaf", "tensor", None, None),
    )
    out_specs = P("leaf", None, "tensor")
    return jax.shard_map(local, mesh=mesh, in_specs=in_specs, out_specs=out_specs, check_vma=False)
```

time: 130 us -> 56.2 us (0.43)
  waiting for transfers between devices: 49.6 us -> 0 us
  Pallas kernels: 0 us -> 48 us
  starting transfers between devices: 31.2 us -> 0 us
  matrix products: 27.6 us -> 0 us
  other arithmetic: 8.15 us -> 0 us
  local copies, waits for them, and re-layouts: 11.4 us -> 7.78 us
    all_to_all x3 -> x0, waiting for transfers between devices: 49.6 us -> none  [the longest x1 22.5 us: local(): lax.all_to_all(spread_heads(trunk_kv, tensor_count, query_heads, group_si...]
    pallas_call x0 -> x1, Pallas kernels: none -> 48 us  [local(): pl.pallas_call(kernel, out_shape=jax.ShapeDtypeStruct((BR, HEADS * HD), j...]
    all_to_all x3 -> x0, starting transfers between devices: 31.2 us -> none  [the longest x1 15.3 us: local(): lax.all_to_all(trunk_mid, 'leaf', split_axis=0, concat_axis=1, tiled=True)]
    dot_general x15 -> x0, matrix products: 27.6 us -> none  [the longest x4 13.6 us: block_step(): jnp.einsum('kgrn,nkd->kgrd', block_weights.astype(jnp.bfloat16), key_piec...]
    gather x5 -> x0, local copies, waits for them, and re-layouts: 7.6 us -> none  [the longest x3 6.29 us: spread_heads(): chosen = jnp.take(values, jnp.asarray(head_picks, dtype=jnp.int32), axis=2)]
    unnamed x14 -> x21, local copies, waits for them, and re-layouts: 0.6 us -> 7.78 us
    reduce_sum x5 -> x0, other arithmetic: 3.36 us -> none  [the longest x4 2.84 us: block_step(): jnp.sum(block_weights, axis=-1)]
    lt x4 -> x0, other arithmetic: 2.51 us -> none  [block_step(): places < length]
  transfers between devices with their start and end apart: 3 -> 0, of which waited for: 3 -> 0; matrix products, arithmetic and copies ran while one was open for 9% -> 0% of each run, Pallas kernels for 0% -> 0%
where the time goes in v1:
time: 56.2 us; the launch traced here: 55.8 us
  Pallas kernels  48 us (85%)
  local copies, waits for them, and re-layouts  7.78 us (14%)
    pallas_call x1, Pallas kernels, local(): pl.pallas_call(kernel, out_shape=jax.ShapeDtypeStruct((BR, HEADS * HD), j...  48 us
    unnamed x21, local copies, waits for them, and re-layouts  7.78 us

profile of v1, /device:TPU:1, one launch (start us, length us, event | category | flops | bytes accessed | tf_op | source)
XLA Modules:
  0.0 55.8 jit_solution(5564073957899083269)
XLA Ops:
  0.0 0.0 copy-start.7
  0.0 0.0 copy-start.8
  0.0 0.0 copy-start.9
  0.0 0.7 %copy-done.7 = s32[1,384]{1,0:T(1,128)S(1)} copy-done((s32[1,384]{1,0:T(1,128)S(1)}, s32[1,384]{1,0:T(1,128)}, u32[]{:S(2)}) %copy-start.7) | copy-done | bytes 1560
  0.7 0.0 copy-done.8
  0.7 0.0 copy-done.9
  0.7 0.0 copy-start
  0.7 1.0 %copy-done = bf16[32,4,8,256]{3,2,1,0:T(8,128)(2,1)S(1)} copy-done((bf16[32,4,8,256]{3,2,1,0:T(8,128)(2,1)S(1)}, bf16[32,4,8,256]{3,2,1,0:T(8,128)(2,1)}, u32[]{:S(2)}) %copy-start) | copy-done | bytes 524312
  1.7 0.0 copy-start.1
  1.7 1.0 %copy-done.1 = bf16[1,384,512]{2,1,0:T(8,128)(2,1)S(1)} copy-done((bf16[1,384,512]{2,1,0:T(8,128)(2,1)S(1)}, bf16[1,384,512]{2,1,0:T(8,128)(2,1)}, u32[]{:S(2)}) %copy-start.1) | copy-done | bytes 393240
  2.7 0.0 copy-start.2
  2.7 1.0 %copy-done.2 = bf16[384,384]{1,0:T(8,128)(2,1)S(1)} copy-done((bf16[384,384]{1,0:T(8,128)(2,1)S(1)}, bf16[384,384]{1,0:T(8,128)(2,1)}, u32[]{:S(2)}) %copy-start.2) | copy-done | bytes 294936
  3.7 0.0 copy-start.3
  3.7 0.9 %copy-done.3 = bf16[256,256]{1,0:T(8,128)(2,1)S(1)} copy-done((bf16[256,256]{1,0:T(8,128)(2,1)S(1)}, bf16[256,256]{1,0:T(8,128)(2,1)}, u32[]{:S(2)}) %copy-start.3) | copy-done | bytes 131096
  4.6 0.0 copy-start.4
  4.6 0.9 %copy-done.4 = bf16[1,24,8,256]{3,2,1,0:T(8,128)(2,1)S(1)} copy-done((bf16[1,24,8,256]{3,2,1,0:T(8,128)(2,1)S(1)}, bf16[1,24,8,256]{3,2,1,0:T(8,128)(2,1)}, u32[]{:S(2)}) %copy-start.4) | copy-done | bytes 98328
  5.5 0.0 copy-start.5
  5.5 0.8 %copy-done.5 = bf16[2,96,96]{2,1,0:T(8,128)(2,1)S(1)} copy-done((bf16[2,96,96]{2,1,0:T(8,128)(2,1)S(1)}, bf16[2,96,96]{2,1,0:T(8,128)(2,1)}, u32[]{:S(2)}) %copy-start.5) | copy-done | bytes 36888
  6.3 0.0 copy-start.6
  6.3 0.8 %copy-done.6 = bf16[128,128]{1,0:T(8,128)(2,1)S(1)} copy-done((bf16[128,128]{1,0:T(8,128)(2,1)S(1)}, bf16[128,128]{1,0:T(8,128)(2,1)}, u32[]{:S(2)}) %copy-start.6) | copy-done | bytes 32792
  7.0 48.0 %shard_map.100 = bf16[384,512]{1,0:T(8,128)(2,1)S(1)} custom-call(s32[32]{0:T(128)S(1)} %copy-done.8, s32[32]{0:T(128)S(1)} %copy-done.9, bf16[32,32,256]{2,1,0:T(8,128)(2,1)S(1)} %bitcast.5, bf16[192,256]{1,0:T(8,128)(2,1)S(1)} %bitcast.7, bf16[384,512]{1,0:T(8,128)(2,1)S(1)} %bitcast.6, s32[1,384]{1,0:T(1,128)S(1)} %copy-done.7, ...), custom_call_target="tpu_custom_call" | custom-call | tf_op jit(solution)/shard_map/pallas_call | solution.py:286
  55.0 0.7 %copy.12 = bf16[1,384,512]{2,1,0:T(8,128)(2,1)} copy(bf16[1,384,512]{2,1,0:T(8,128)(2,1)S(1)} %bitcast.4) | data formatting | bytes 786432
Async XLA Ops:
  0.0 0.7 %copy-start.7 = (s32[1,384]{1,0:T(1,128)S(1)}, s32[1,384]{1,0:T(1,128)}, u32[]{:S(2)}) copy-start(s32[1,384]{1,0:T(1,128)} %parents.1) | copy-start | bytes 4612
  0.0 0.7 %copy-start.8 = (s32[32]{0:T(128)S(1)}, s32[32]{0:T(128)}, u32[]{:S(2)}) copy-start(s32[32]{0:T(128)} %slots.1) | copy-start | bytes 388
  0.0 0.7 %copy-start.9 = (s32[32]{0:T(128)S(1)}, s32[32]{0:T(128)}, u32[]{:S(2)}) copy-start(s32[32]{0:T(128)} %lengths.1) | copy-start | bytes 388
  0.7 1.0 %copy-start = (bf16[32,4,8,256]{3,2,1,0:T(8,128)(2,1)S(1)}, bf16[32,4,8,256]{3,2,1,0:T(8,128)(2,1)}, u32[]{:S(2)}) copy-start(bf16[32,4,8,256]{3,2,1,0:T(8,128)(2,1)} %param.10) | copy-start | bytes 1572868
  1.7 1.0 %copy-start.1 = (bf16[1,384,512]{2,1,0:T(8,128)(2,1)S(1)}, bf16[1,384,512]{2,1,0:T(8,128)(2,1)}, u32[]{:S(2)}) copy-start(bf16[1,384,512]{2,1,0:T(8,128)(2,1)} %param.14) | copy-start | bytes 1179652
  2.7 1.0 %copy-start.2 = (bf16[384,384]{1,0:T(8,128)(2,1)S(1)}, bf16[384,384]{1,0:T(8,128)(2,1)}, u32[]{:S(2)}) copy-start(bf16[384,384]{1,0:T(8,128)(2,1)} %constant.10.clone.pick_out) | copy-start | bytes 884740
  3.7 0.9 %copy-start.3 = (bf16[256,256]{1,0:T(8,128)(2,1)S(1)}, bf16[256,256]{1,0:T(8,128)(2,1)}, u32[]{:S(2)}) copy-start(bf16[256,256]{1,0:T(8,128)(2,1)} %constant.9.clone.pick_target) | copy-start | bytes 393220
  4.6 0.9 %copy-start.4 = (bf16[1,24,8,256]{3,2,1,0:T(8,128)(2,1)S(1)}, bf16[1,24,8,256]{3,2,1,0:T(8,128)(2,1)}, u32[]{:S(2)}) copy-start(bf16[1,24,8,256]{3,2,1,0:T(8,128)(2,1)} %param.15) | copy-start | bytes 294916
  5.5 0.8 %copy-start.5 = (bf16[2,96,96]{2,1,0:T(8,128)(2,1)S(1)}, bf16[2,96,96]{2,1,0:T(8,128)(2,1)}, u32[]{:S(2)}) copy-start(bf16[2,96,96]{2,1,0:T(8,128)(2,1)} %constant.11.clone.pick_in) | copy-start | bytes 110596
  6.3 0.8 %copy-start.6 = (bf16[128,128]{1,0:T(8,128)(2,1)S(1)}, bf16[128,128]{1,0:T(8,128)(2,1)}, u32[]{:S(2)}) copy-start(bf16[128,128]{1,0:T(8,128)(2,1)} %constant.8.clone.pick_head) | copy-start | bytes 98308

commit v2 on v1

v2 whole, which is shorter than its diff:
```python
import math

import jax
import jax.numpy as jnp
from jax import lax
from jax.experimental import pallas as pl
from jax.experimental.pallas import tpu as pltpu
from jax.sharding import PartitionSpec as P

MESH = pl.DeviceIdType.MESH

HD = 128
BR = 384
TREES = 32
HEADS = 4
PAIRS = 2
WIDE = 2 * BR
NZ = 8
NY = 8
CHUNKS = 4
DEAD = -1e30
SCORE_SCALE = math.log2(math.e) / math.sqrt(HD)


def picks(target, rows, columns):
    row = lax.broadcasted_iota(jnp.int32, (rows, columns), 0)
    column = lax.broadcasted_iota(jnp.int32, (rows, columns), 1)
    return jnp.where(row == target(column), 1.0, 0.0).astype(jnp.bfloat16)


def moved(order, rows):
    return jnp.dot(order, rows, preferred_element_type=jnp.float32).astype(jnp.bfloat16)


def kernel(
    slots, lengths, trunk_hbm, branch_hbm, queries_hbm, parents_hbm,
    out,
    trunk, branch, queries, parents, pick_head, pick_target,
    staged, landed, sorted_rows, keys_values, branch_staged, branch_landed, branch_kv,
    turned, shown, top, total, summed,
    load, send_a, recv_a, send_b, recv_b, recv_c, send_f, recv_f, send_r, recv_r, send_p, recv_p,
):
    leaf = lax.axis_index("leaf")
    tensor = lax.axis_index("tensor")
    xh, z, c = leaf // 16, (leaf // 2) % 8, leaf % 2
    y, xl = tensor // 2, tensor % 2

    loads = [
        pltpu.make_async_copy(far, near, load.at[which])
        for which, (far, near) in enumerate(
            [(trunk_hbm, trunk), (branch_hbm, branch), (parents_hbm, parents), (queries_hbm, queries)]
        )
    ]
    for one in loads:
        one.start()

    def place(xh, z, c, y, xl):
        return ((xh * 8 + z) * 2 + c, y * 2 + xl)

    def near(a, d, b):
        return place((xh + a) % 2, z, (c + b) % 2, y, (xl + d) % 2)

    barrier = pltpu.get_barrier_semaphore()
    direct = ((1, 1, 0), (1, 1, 1), (0, 1, 0), (0, 1, 1), (0, 0, 1))

    def greet(step, _):
        pl.semaphore_signal(
            barrier, inc=1, device_id=place(xh, (z + step // 8) % 8, c, (y + step % 8) % 8, xl),
            device_id_type=MESH,
        )
        return 0

    lax.fori_loop(1, NZ * NY, greet, 0)
    for flips in direct:
        pl.semaphore_signal(barrier, inc=1, device_id=near(*flips), device_id_type=MESH)

    pick_head[...] = picks(
        lambda i: (i & 7) * 16 + (i >> 5) * 4 + ((i >> 3) & 3), 128, 128
    )
    pick_target[...] = picks(
        lambda i: ((i >> 2) & 3) * 64 + (i >> 4) * 4 + (i & 3), 256, 256
    )

    def z_offset(chunk, member):
        return (chunk + 1) % 4 if member == 0 else 7 - chunk

    def stage(chunk):
        for member in range(2):
            z_to = (z + z_offset(chunk, member)) % 8
            rows = jnp.concatenate(
                [trunk[slots[((q // 2) * 8 + z_to) * 2 + q % 2]] for q in range(4)], axis=0
            )
            ordered = moved(pick_head[...], rows)
            for head in range(8):
                staged[chunk * 2 + member, head] = ordered[head * 16 : head * 16 + 16]

    def send_plane(chunk):
        for dy in (4, 3, 5, 2, 6, 1, 7, 0):
            y_to = (y + dy) % 8
            for member in range(2):
                group = chunk * 2 + member
                z_to = (z + z_offset(chunk, member)) % 8

                def send():
                    pltpu.make_async_remote_copy(
                        src_ref=staged.at[group, y_to],
                        dst_ref=landed.at[group * 8 + dy],
                        send_sem=send_a,
                        recv_sem=recv_a.at[chunk],
                        device_id=place(xh, z_to, c, y_to, xl),
                        device_id_type=MESH,
                    ).start()

                if dy == 0 and member == 0:
                    pl.when(chunk != 3)(send)
                else:
                    send()

    def stage_and_send(chunk, _):
        stage(chunk)
        send_plane(chunk)
        return 0

    loads[0].wait()
    pl.semaphore_wait(barrier, NZ * NY - 1 + len(direct))
    lax.fori_loop(0, 2, stage_and_send, 0)

    loads[1].wait()

    def branch_target(i):
        half = jnp.where(i >= 192, 1, 0)
        inner = i - 192 * half
        return (inner & 7) * 48 + half * 24 + (inner >> 3)

    rows = jnp.concatenate([branch[:, :HD], branch[:, HD:]], axis=0)
    ordered = moved(picks(branch_target, 384, 384), rows)
    for head in range(8):
        branch_staged[head] = ordered[head * 48 : head * 48 + 48]
    for dy in (4, 3, 5, 2, 6, 1, 7):
        y_to = (y + dy) % 8
        pltpu.make_async_remote_copy(
            src_ref=branch_staged.at[y_to],
            dst_ref=branch_landed.at[0, dy],
            send_sem=send_r,
            recv_sem=recv_r,
            device_id=place(xh, z, c, y_to, xl),
            device_id_type=MESH,
        ).start()
    branch_landed[0, 0] = branch_staged[y]

    def wait_bytes(ref, sem):
        pltpu.make_async_copy(ref, ref, sem).wait()

    def pass_on(chunk):
        if chunk < 3:
            wait_bytes(landed.at[chunk * 16 : chunk * 16 + 16], recv_a.at[chunk])
        else:
            wait_bytes(landed.at[49:64], recv_a.at[chunk])
        rows = landed[chunk * 16 : chunk * 16 + 16].reshape(256, 256)
        ordered = moved(pick_target[...], rows)
        for target in range(4):
            sorted_rows[chunk, target] = ordered[target * 64 : target * 64 + 64]
        for a, d, b in direct:
            target = ((xh + a) % 2) * 2 + (c + b) % 2
            pltpu.make_async_remote_copy(
                src_ref=sorted_rows.at[chunk, target],
                dst_ref=keys_values.at[chunk, a * 4 + d * 2 + b],
                send_sem=send_b,
                recv_sem=recv_c.at[chunk] if a else recv_b.at[chunk],
                device_id=near(a, d, b),
                device_id_type=MESH,
            ).start()
        keys_values[chunk, 0] = sorted_rows[chunk, xh * 2 + c]

    def hand_on(chunk):
        wait_bytes(keys_values.at[chunk, 6:8], recv_c.at[chunk])
        pltpu.make_async_remote_copy(
            src_ref=keys_values.at[chunk, 6:8],
            dst_ref=keys_values.at[chunk, 4:6],
            send_sem=send_f,
            recv_sem=recv_f.at[chunk],
            device_id=near(0, 1, 0),
            device_id_type=MESH,
        ).start()

    def attend(keys, values, mask, first):
        keys = jnp.concatenate([keys, keys], axis=1)
        values = jnp.transpose(values)
        mask = jnp.concatenate([mask] * (WIDE // mask.shape[1]), axis=1)
        for pair in range(PAIRS):
            scores = jnp.dot(keys, turned[pair], preferred_element_type=jnp.float32) + mask
            best = jnp.max(scores, axis=0, keepdims=True)
            if not first:
                best = jnp.maximum(best, top[pair])
            weights = jnp.exp2(scores - best)
            weight_sum = jnp.sum(weights, axis=0, keepdims=True)
            product = jnp.dot(
                values, weights.astype(jnp.bfloat16), preferred_element_type=jnp.float32
            )
            if first:
                total[pair] = weight_sum
                summed[pair] = product
            else:
                fade = jnp.exp2(top[pair] - best)
                total[pair] = total[pair] * fade + weight_sum
                summed[pair] = summed[pair] * fade + product
            top[pair] = best

    def attend_chunk(chunk):
        wait_bytes(keys_values.at[chunk, 1:4], recv_b.at[chunk])
        wait_bytes(keys_values.at[chunk, 4:6], recv_f.at[chunk])
        both = keys_values[chunk].reshape(512, 256)
        key = lax.broadcasted_iota(jnp.int32, (512, HD), 0)
        xh_from = (xh + (key >> 8)) & 1
        xl_from = (xl + (key >> 7)) & 1
        c_from = (c + (key >> 6)) & 1
        dz = jnp.where(((key >> 5) & 1) == 0, (chunk + 1) % 4, 7 - chunk)
        z_from = (z - dz + 8) & 7
        y_from = (y - ((key >> 2) & 7) + 8) & 7
        position = (((xh_from * 8 + z_from) * 2 + c_from) * 16 + y_from * 2 + xl_from) * 4 + (key & 3)
        mask = jnp.where(position < lengths[slots[leaf]], 0.0, DEAD)
        attend(both[:, :HD], both[:, HD:], mask, False)

    def attend_branch():
        wait_bytes(branch_landed.at[1], recv_p)

        def target(i):
            other = jnp.where(i >= 48, 1, 0)
            inner = i - 48 * other
            half = jnp.where(inner >= 24, 1, 0)
            return half * 48 + ((other + xl) & 1) * 24 + inner - 24 * half

        order = picks(target, 96, 96)
        for dy in range(8):
            y_from = (y - dy + 8) % 8
            rows = jnp.concatenate([branch_landed[0, dy], branch_landed[1, dy]], axis=0)
            ordered = moved(order, rows)
            branch_kv[0, y_from] = ordered[:48]
            branch_kv[1, y_from] = ordered[48:]
        attend(branch_kv[0].reshape(BR, HD), branch_kv[1].reshape(BR, HD), shown[...], True)

    def turn_queries():
        loads[3].wait()
        for head in range(HEADS):
            flipped = jnp.transpose(queries[:, head * HD : head * HD + HD])
            scaled = flipped.astype(jnp.float32) * SCORE_SCALE
            coarse = scaled.astype(jnp.bfloat16)
            fine = (scaled - coarse.astype(jnp.float32)).astype(jnp.bfloat16)
            columns = slice((head % 2) * BR, (head % 2) * BR + BR)
            turned[head // 2, :HD, columns] = coarse
            turned[head // 2, HD:, columns] = fine

    def mark_ancestors():
        loads[2].wait()
        above = lax.broadcasted_iota(jnp.int32, (HD, HD), 0)
        along = lax.broadcasted_iota(jnp.int32, (HD, HD), 1)

        def links(up, down):
            return above + up * HD == parents[:, down * HD : down * HD + HD]

        def as_picks(wanted):
            return jnp.where(wanted, 1.0, 0.0).astype(jnp.bfloat16)

        within = [as_picks(jnp.logical_or(links(b, b), above == along)) for b in range(3)]
        for _ in range(7):
            within = [
                as_picks(jnp.dot(one, one, preferred_element_type=jnp.float32) > 0.5)
                for one in within
            ]
        step_one = moved(as_picks(links(0, 1)), within[1])
        step_two = moved(as_picks(links(1, 2)), within[2])
        zero_one = moved(within[0], step_one)
        blocks = {
            (0, 0): within[0], (1, 1): within[1], (2, 2): within[2],
            (0, 1): zero_one, (1, 2): moved(within[1], step_two), (0, 2): moved(zero_one, step_two),
        }
        for up in range(3):
            for down in range(3):
                if (up, down) in blocks:
                    mask = jnp.where(blocks[up, down].astype(jnp.float32) > 0.5, 0.0, DEAD)
                else:
                    mask = jnp.full((HD, HD), DEAD, jnp.float32)
                shown[up * HD : up * HD + HD, down * HD : down * HD + HD] = mask

    lax.fori_loop(2, 3, stage_and_send, 0)
    pass_on(0)
    lax.fori_loop(3, 4, stage_and_send, 0)
    landed[48] = staged[6, y]
    pass_on(1)
    hand_on(0)
    turn_queries()
    wait_bytes(branch_landed.at[0, 1:8], recv_r)
    pltpu.make_async_remote_copy(
        src_ref=branch_landed.at[0],
        dst_ref=branch_landed.at[1],
        send_sem=send_p,
        recv_sem=recv_p,
        device_id=near(0, 1, 0),
        device_id_type=MESH,
    ).start()
    mark_ancestors()
    pass_on(2)
    hand_on(1)
    attend_branch()
    pass_on(3)
    hand_on(2)
    attend_chunk(0)
    hand_on(3)
    attend_chunk(1)
    attend_chunk(2)
    attend_chunk(3)

    for head in range(HEADS):
        columns = slice((head % 2) * BR, (head % 2) * BR + BR)
        result = summed[head // 2, :, columns] * (1.0 / total[head // 2, :, columns])
        out[:, head * HD : head * HD + HD] = jnp.transpose(result.astype(jnp.bfloat16))

    wait_bytes(landed.at[1:64], send_a)
    wait_bytes(branch_landed.at[0, 1:8], send_r)
    wait_bytes(branch_landed.at[0], send_p)
    wait_bytes(keys_values.at[:, 0:5], send_b)
    wait_bytes(keys_values.at[:, 0:2], send_f)


def local(trunk_kv, slot_trees, trunk_len, parents, queries, branch_kv):
    smem = pl.BlockSpec(memory_space=pltpu.SMEM)
    hbm = pl.BlockSpec(memory_space=pltpu.HBM)
    bf16, f32 = jnp.bfloat16, jnp.float32
    attended = pl.pallas_call(
        kernel,
        out_shape=jax.ShapeDtypeStruct((BR, HEADS * HD), bf16),
        in_specs=[smem, smem, hbm, hbm, hbm, hbm],
        out_specs=pl.BlockSpec(memory_space=pltpu.VMEM),
        scratch_shapes=[
            pltpu.VMEM((TREES, 32, 256), bf16),
            pltpu.VMEM((192, 256), bf16),
            pltpu.VMEM((BR, HEADS * HD), bf16),
            pltpu.VMEM((1, BR), jnp.int32),
            pltpu.VMEM((128, 128), bf16),
            pltpu.VMEM((256, 256), bf16),
            pltpu.VMEM((8, 8, 16, 256), bf16),
            pltpu.VMEM((64, 16, 256), bf16),
            pltpu.VMEM((CHUNKS, 4, 64, 256), bf16),
            pltpu.VMEM((CHUNKS, 8, 64, 256), bf16),
            pltpu.VMEM((8, 48, HD), bf16),
            pltpu.VMEM((2, 8, 48, HD), bf16),
            pltpu.VMEM((2, 8, 48, HD), bf16),
            pltpu.VMEM((PAIRS, 2 * HD, WIDE), bf16),
            pltpu.VMEM((BR, BR), f32),
            pltpu.VMEM((PAIRS, 1, WIDE), f32),
            pltpu.VMEM((PAIRS, 1, WIDE), f32),
            pltpu.VMEM((PAIRS, HD, WIDE), f32),
            pltpu.SemaphoreType.DMA((4,)),
            pltpu.SemaphoreType.DMA,
            pltpu.SemaphoreType.DMA((CHUNKS,)),
            pltpu.SemaphoreType.DMA,
            pltpu.SemaphoreType.DMA((CHUNKS,)),
            pltpu.SemaphoreType.DMA((CHUNKS,)),
            pltpu.SemaphoreType.DMA,
            pltpu.SemaphoreType.DMA((CHUNKS,)),
            pltpu.SemaphoreType.DMA,
            pltpu.SemaphoreType.DMA,
            pltpu.SemaphoreType.DMA,
            pltpu.SemaphoreType.DMA,
        ],
        compiler_params=pltpu.CompilerParams(
            collective_id=0, has_side_effects=True, vmem_limit_bytes=60 * 1024 * 1024
        ),
    )(
        slot_trees,
        trunk_len,
        trunk_kv.reshape(TREES, 32, 2 * HD),
        branch_kv.reshape(192, 2 * HD),
        queries.reshape(BR, HEADS * HD),
        parents,
    )
    return attended.reshape(1, BR, HEADS * HD)


def solution(mesh):
    in_specs = (
        P(None, ("leaf", "tensor"), None, None),
        P(),
        P(),
        P("leaf", None),
        P("leaf", None, "tensor"),
        P("leaf", "tensor", None, None),
    )
    out_specs = P("leaf", None, "tensor")
    return jax.shard_map(local, mesh=mesh, in_specs=in_specs, out_specs=out_specs, check_vma=False)
```

time: 56.2 us -> 48.2 us (0.86)
  local copies, waits for them, and re-layouts: 7.78 us -> 1.77 us
  Pallas kernels: 48 us -> 46.3 us
    unnamed x21 -> x1, local copies, waits for them, and re-layouts: 7.78 us -> 1.77 us
    pallas_call x1, Pallas kernels: 48 us -> 46.3 us  [local(): pl.pallas_call(kernel, out_shape=jax.ShapeDtypeStruct((BR, HEADS * HD), b...]
where the time goes in v2:
time: 48.2 us; the launch traced here: 48.1 us
  Pallas kernels  46.3 us (96%)
  local copies, waits for them, and re-layouts  1.77 us (4%)
    pallas_call x1, Pallas kernels, local(): pl.pallas_call(kernel, out_shape=jax.ShapeDtypeStruct((BR, HEADS * HD), b...  46.3 us
    unnamed x1, local copies, waits for them, and re-layouts  1.77 us

profile of v2, /device:TPU:1, one launch (start us, length us, event | category | flops | bytes accessed | tf_op | source)
XLA Modules:
  0.0 48.1 jit_solution(3348703893563554156)
XLA Ops:
  0.0 46.3 %shard_map.64 = bf16[384,512]{1,0:T(8,128)(2,1)} custom-call(s32[32]{0:T(128)} %slots.1, s32[32]{0:T(128)} %lengths.1, bf16[32,32,256]{2,1,0:T(8,128)(2,1)} %bitcast.5, bf16[192,256]{1,0:T(8,128)(2,1)} %bitcast.7, bf16[384,512]{1,0:T(8,128)(2,1)} %bitcast.6, s32[1,384]{1,0:T(1,128)} %parents_hbm.1), custom_call_target="tpu_custom_call" | custom-call | tf_op jit(solution)/shard_map/pallas_call | solution.py:329
  46.3 1.8 %copy.8 = bf16[1,384,512]{2,1,0:T(8,128)(2,1)} copy(bf16[1,384,512]{2,1,0:T(8,128)(2,1)} %bitcast.4) | data formatting | bytes 786432

commit v3 on v2

--- a/solution.py
+++ b/solution.py
@@ -15,9 +15,8 @@
 HEADS = 4
 PAIRS = 2
 WIDE = 2 * BR
-NZ = 8
-NY = 8
 CHUNKS = 4
+OFFSETS = ((4, 7), (3, 5), (2, 6), (1, 0))
 DEAD = -1e30
 SCORE_SCALE = math.log2(math.e) / math.sqrt(HD)
 
@@ -36,9 +35,9 @@
     slots, lengths, trunk_hbm, branch_hbm, queries_hbm, parents_hbm,
     out,
     trunk, branch, queries, parents, pick_head, pick_target,
-    staged, landed, sorted_rows, keys_values, branch_staged, branch_landed, branch_kv,
-    turned, shown, top, total, summed,
-    load, send_a, recv_a, send_b, recv_b, recv_c, send_f, recv_f, send_r, recv_r, send_p, recv_p,
+    staged, row_landed, plane_landed, sorted_rows, keys_values, branch_staged, branch_landed, branch_kv,
+    turned, shown, top, total, summed, result,
+    load, send_y, recv_y, send_z, recv_z, send_b, recv_b, recv_c, send_f, recv_f, send_r, recv_r, send_p, recv_p, store,
 ):
     leaf = lax.axis_index("leaf")
     tensor = lax.axis_index("tensor")
@@ -46,8 +45,8 @@
     y, xl = tensor // 2, tensor % 2
 
     loads = [
-        pltpu.make_async_copy(far, near, load.at[which])
-        for which, (far, near) in enumerate(
+        pltpu.make_async_copy(there, here, load.at[which])
+        for which, (there, here) in enumerate(
             [(trunk_hbm, trunk), (branch_hbm, branch), (parents_hbm, parents), (queries_hbm, queries)]
         )
     ]
@@ -63,16 +62,14 @@
     barrier = pltpu.get_barrier_semaphore()
     direct = ((1, 1, 0), (1, 1, 1), (0, 1, 0), (0, 1, 1), (0, 0, 1))
 
-    def greet(step, _):
-        pl.semaphore_signal(
-            barrier, inc=1, device_id=place(xh, (z + step // 8) % 8, c, (y + step % 8) % 8, xl),
-            device_id_type=MESH,
-        )
-        return 0
-
-    lax.fori_loop(1, NZ * NY, greet, 0)
+    def signal(where):
+        pl.semaphore_signal(barrier, inc=1, device_id=where, device_id_type=MESH)
+
+    for step in range(1, 8):
+        signal(place(xh, z, c, (y + step) % 8, xl))
+        signal(place(xh, (z + step) % 8, c, y, xl))
     for flips in direct:
-        pl.semaphore_signal(barrier, inc=1, device_id=near(*flips), device_id_type=MESH)
+        signal(near(*flips))
 
     pick_head[...] = picks(
         lambda i: (i & 7) * 16 + (i >> 5) * 4 + ((i >> 3) & 3), 128, 128
@@ -81,49 +78,32 @@
         lambda i: ((i >> 2) & 3) * 64 + (i >> 4) * 4 + (i & 3), 256, 256
     )
 
-    def z_offset(chunk, member):
-        return (chunk + 1) % 4 if member == 0 else 7 - chunk
-
-    def stage(chunk):
-        for member in range(2):
-            z_to = (z + z_offset(chunk, member)) % 8
+    def send_row(chunk):
+        for member, dz in enumerate(OFFSETS[chunk]):
+            z_to = (z + dz) % 8
             rows = jnp.concatenate(
                 [trunk[slots[((q // 2) * 8 + z_to) * 2 + q % 2]] for q in range(4)], axis=0
             )
             ordered = moved(pick_head[...], rows)
             for head in range(8):
-                staged[chunk * 2 + member, head] = ordered[head * 16 : head * 16 + 16]
-
-    def send_plane(chunk):
-        for dy in (4, 3, 5, 2, 6, 1, 7, 0):
+                staged[chunk, head, member] = ordered[head * 16 : head * 16 + 16]
+        for dy in (4, 3, 5, 2, 6, 1, 7):
             y_to = (y + dy) % 8
-            for member in range(2):
-                group = chunk * 2 + member
-                z_to = (z + z_offset(chunk, member)) % 8
-
-                def send():
-                    pltpu.make_async_remote_copy(
-                        src_ref=staged.at[group, y_to],
-                        dst_ref=landed.at[group * 8 + dy],
-                        send_sem=send_a,
-                        recv_sem=recv_a.at[chunk],
-                        device_id=place(xh, z_to, c, y_to, xl),
-                        device_id_type=MESH,
-                    ).start()
-
-                if dy == 0 and member == 0:
-                    pl.when(chunk != 3)(send)
-                else:
-                    send()
-
-    def stage_and_send(chunk, _):
-        stage(chunk)
-        send_plane(chunk)
-        return 0
+            pltpu.make_async_remote_copy(
+                src_ref=staged.at[chunk, y_to],
+                dst_ref=row_landed.at[chunk, :, dy],
+                send_sem=send_y,
+                recv_sem=recv_y.at[chunk],
+                device_id=place(xh, z, c, y_to, xl),
+                device_id_type=MESH,
+            ).start()
+        for member in range(2):
+            row_landed[chunk, member, 0] = staged[chunk, y, member]
 
     loads[0].wait()
-    pl.semaphore_wait(barrier, NZ * NY - 1 + len(direct))
-    lax.fori_loop(0, 2, stage_and_send, 0)
+    pl.semaphore_wait(barrier, 14 + len(direct))
+    send_row(0)
+    send_row(1)
 
     loads[1].wait()
 
@@ -151,12 +131,28 @@
     def wait_bytes(ref, sem):
         pltpu.make_async_copy(ref, ref, sem).wait()
 
+    def send_plane(chunk):
+        wait_bytes(row_landed.at[chunk, :, 1:8], recv_y.at[chunk])
+        for member, dz in enumerate(OFFSETS[chunk]):
+            if dz:
+                pltpu.make_async_remote_copy(
+                    src_ref=row_landed.at[chunk, member],
+                    dst_ref=plane_landed.at[chunk * 2 + member],
+                    send_sem=send_z,
+                    recv_sem=recv_z.at[chunk],
+                    device_id=place(xh, (z + dz) % 8, c, y, xl),
+                    device_id_type=MESH,
+                ).start()
+
     def pass_on(chunk):
         if chunk < 3:
-            wait_bytes(landed.at[chunk * 16 : chunk * 16 + 16], recv_a.at[chunk])
+            wait_bytes(plane_landed.at[chunk * 2 : chunk * 2 + 2], recv_z.at[chunk])
+            rows = plane_landed[chunk * 2 : chunk * 2 + 2].reshape(256, 256)
         else:
-            wait_bytes(landed.at[49:64], recv_a.at[chunk])
-        rows = landed[chunk * 16 : chunk * 16 + 16].reshape(256, 256)
+            wait_bytes(plane_landed.at[6], recv_z.at[chunk])
+            rows = jnp.concatenate(
+                [plane_landed[6].reshape(128, 256), row_landed[3, 1].reshape(128, 256)], axis=0
+            )
         ordered = moved(pick_target[...], rows)
         for target in range(4):
             sorted_rows[chunk, target] = ordered[target * 64 : target * 64 + 64]
@@ -214,7 +210,7 @@
         xh_from = (xh + (key >> 8)) & 1
         xl_from = (xl + (key >> 7)) & 1
         c_from = (c + (key >> 6)) & 1
-        dz = jnp.where(((key >> 5) & 1) == 0, (chunk + 1) % 4, 7 - chunk)
+        dz = jnp.where(((key >> 5) & 1) == 0, OFFSETS[chunk][0], OFFSETS[chunk][1])
         z_from = (z - dz + 8) & 7
         y_from = (y - ((key >> 2) & 7) + 8) & 7
         position = (((xh_from * 8 + z_from) * 2 + c_from) * 16 + y_from * 2 + xl_from) * 4 + (key & 3)
@@ -282,13 +278,12 @@
                     mask = jnp.full((HD, HD), DEAD, jnp.float32)
                 shown[up * HD : up * HD + HD, down * HD : down * HD + HD] = mask
 
-    lax.fori_loop(2, 3, stage_and_send, 0)
+    send_plane(0)
+    send_row(2)
+    send_row(3)
+    send_plane(1)
+    turn_queries()
     pass_on(0)
-    lax.fori_loop(3, 4, stage_and_send, 0)
-    landed[48] = staged[6, y]
-    pass_on(1)
-    hand_on(0)
-    turn_queries()
     wait_bytes(branch_landed.at[0, 1:8], recv_r)
     pltpu.make_async_remote_copy(
         src_ref=branch_landed.at[0],
@@ -299,23 +294,34 @@
         device_id_type=MESH,
     ).start()
     mark_ancestors()
+    pass_on(1)
+    hand_on(0)
+    send_plane(2)
+    attend_branch()
+    hand_on(1)
     pass_on(2)
-    hand_on(1)
-    attend_branch()
+    send_plane(3)
+    attend_chunk(0)
     pass_on(3)
     hand_on(2)
-    attend_chunk(0)
+    attend_chunk(1)
     hand_on(3)
-    attend_chunk(1)
     attend_chunk(2)
     attend_chunk(3)
 
+    stores = []
     for head in range(HEADS):
         columns = slice((head % 2) * BR, (head % 2) * BR + BR)
-        result = summed[head // 2, :, columns] * (1.0 / total[head // 2, :, columns])
-        out[:, head * HD : head * HD + HD] = jnp.transpose(result.astype(jnp.bfloat16))
-
-    wait_bytes(landed.at[1:64], send_a)
+        lanes = slice(head * HD, head * HD + HD)
+        normal = summed[head // 2, :, columns] * (1.0 / total[head // 2, :, columns])
+        result[:, lanes] = jnp.transpose(normal.astype(jnp.bfloat16))
+        stores.append(pltpu.make_async_copy(result.at[:, lanes], out.at[:, lanes], store.at[head]))
+        stores[-1].start()
+    for one in stores:
+        one.wait()
+
+    wait_bytes(row_landed.at[:, :, 1:8], send_y)
+    wait_bytes(plane_landed.at[0:7], send_z)
     wait_bytes(branch_landed.at[0, 1:8], send_r)
     wait_bytes(branch_landed.at[0], send_p)
     wait_bytes(keys_values.at[:, 0:5], send_b)
@@ -330,7 +336,7 @@
         kernel,
         out_shape=jax.ShapeDtypeStruct((BR, HEADS * HD), bf16),
         in_specs=[smem, smem, hbm, hbm, hbm, hbm],
-        out_specs=pl.BlockSpec(memory_space=pltpu.VMEM),
+        out_specs=hbm,
         scratch_shapes=[
             pltpu.VMEM((TREES, 32, 256), bf16),
             pltpu.VMEM((192, 256), bf16),
@@ -338,8 +344,9 @@
             pltpu.VMEM((1, BR), jnp.int32),
             pltpu.VMEM((128, 128), bf16),
             pltpu.VMEM((256, 256), bf16),
+            pltpu.VMEM((CHUNKS, 8, 2, 16, 256), bf16),
+            pltpu.VMEM((CHUNKS, 2, 8, 16, 256), bf16),
             pltpu.VMEM((8, 8, 16, 256), bf16),
-            pltpu.VMEM((64, 16, 256), bf16),
             pltpu.VMEM((CHUNKS, 4, 64, 256), bf16),
             pltpu.VMEM((CHUNKS, 8, 64, 256), bf16),
             pltpu.VMEM((8, 48, HD), bf16),
@@ -350,7 +357,10 @@
             pltpu.VMEM((PAIRS, 1, WIDE), f32),
             pltpu.VMEM((PAIRS, 1, WIDE), f32),
             pltpu.VMEM((PAIRS, HD, WIDE), f32),
+            pltpu.VMEM((BR, HEADS * HD), bf16),
             pltpu.SemaphoreType.DMA((4,)),
+            pltpu.SemaphoreType.DMA,
+            pltpu.SemaphoreType.DMA((CHUNKS,)),
             pltpu.SemaphoreType.DMA,
             pltpu.SemaphoreType.DMA((CHUNKS,)),
             pltpu.SemaphoreType.DMA,
@@ -362,6 +372,7 @@
             pltpu.SemaphoreType.DMA,
             pltpu.SemaphoreType.DMA,
             pltpu.SemaphoreType.DMA,
+            pltpu.SemaphoreType.DMA((HEADS,)),
         ],
         compiler_params=pltpu.CompilerParams(
             collective_id=0, has_side_effects=True, vmem_limit_bytes=60 * 1024 * 1024

time: 48.2 us -> 52.8 us (1.095)
  Pallas kernels: 46.3 us -> 50.9 us
    pallas_call x1, Pallas kernels: 46.3 us -> 50.9 us  [local(): pl.pallas_call(kernel, out_shape=jax.ShapeDtypeStruct((BR, HEADS * HD), b...]
where the time goes in v3:
time: 52.8 us; the launch traced here: 52.6 us
  Pallas kernels  50.9 us (96%)
  local copies, waits for them, and re-layouts  1.77 us (3%)
    pallas_call x1, Pallas kernels, local(): pl.pallas_call(kernel, out_shape=jax.ShapeDtypeStruct((BR, HEADS * HD), b...  50.9 us
    unnamed x1, local copies, waits for them, and re-layouts  1.77 us

profile of v3, /device:TPU:1, one launch (start us, length us, event | category | flops | bytes accessed | tf_op | source)
XLA Modules:
  0.0 52.6 jit_solution(10799074863004419553)
XLA Ops:
  0.0 50.9 %shard_map.64 = bf16[384,512]{1,0:T(8,128)(2,1)} custom-call(s32[32]{0:T(128)} %slots.1, s32[32]{0:T(128)} %lengths.1, bf16[32,32,256]{2,1,0:T(8,128)(2,1)} %bitcast.5, bf16[192,256]{1,0:T(8,128)(2,1)} %bitcast.7, bf16[384,512]{1,0:T(8,128)(2,1)} %bitcast.6, s32[1,384]{1,0:T(1,128)} %parents_hbm.1), custom_call_target="tpu_custom_call" | custom-call | tf_op jit(solution)/shard_map/pallas_call | solution.py:335
  50.9 1.8 %copy.8 = bf16[1,384,512]{2,1,0:T(8,128)(2,1)} copy(bf16[1,384,512]{2,1,0:T(8,128)(2,1)} %bitcast.4) | data formatting | bytes 786432

commit v4 on v2

--- a/solution.py
+++ b/solution.py
@@ -123,7 +123,7 @@
 
     loads[0].wait()
     pl.semaphore_wait(barrier, NZ * NY - 1 + len(direct))
-    lax.fori_loop(0, 2, stage_and_send, 0)
+    lax.fori_loop(0, 1, stage_and_send, 0)
 
     loads[1].wait()
 
@@ -282,23 +282,27 @@
                     mask = jnp.full((HD, HD), DEAD, jnp.float32)
                 shown[up * HD : up * HD + HD, down * HD : down * HD + HD] = mask
 
+    def hand_branch():
+        wait_bytes(branch_landed.at[0, 1:8], recv_r)
+        pltpu.make_async_remote_copy(
+            src_ref=branch_landed.at[0],
+            dst_ref=branch_landed.at[1],
+            send_sem=send_p,
+            recv_sem=recv_p,
+            device_id=near(0, 1, 0),
+            device_id_type=MESH,
+        ).start()
+
+    lax.fori_loop(1, 2, stage_and_send, 0)
+    turn_queries()
+    pass_on(0)
     lax.fori_loop(2, 3, stage_and_send, 0)
-    pass_on(0)
+    mark_ancestors()
+    pass_on(1)
     lax.fori_loop(3, 4, stage_and_send, 0)
     landed[48] = staged[6, y]
-    pass_on(1)
     hand_on(0)
-    turn_queries()
-    wait_bytes(branch_landed.at[0, 1:8], recv_r)
-    pltpu.make_async_remote_copy(
-        src_ref=branch_landed.at[0],
-        dst_ref=branch_landed.at[1],
-        send_sem=send_p,
-        recv_sem=recv_p,
-        device_id=near(0, 1, 0),
-        device_id_type=MESH,
-    ).start()
-    mark_ancestors()
+    hand_branch()
     pass_on(2)
     hand_on(1)
     attend_branch()

time: 48.2 us -> 50.6 us (1.050)
  Pallas kernels: 46.3 us -> 48.7 us
    pallas_call x1, Pallas kernels: 46.3 us -> 48.7 us  [local(): pl.pallas_call(kernel, out_shape=jax.ShapeDtypeStruct((BR, HEADS * HD), b...]
where the time goes in v4:
time: 50.6 us; the launch traced here: 50.5 us
  Pallas kernels  48.7 us (96%)
  local copies, waits for them, and re-layouts  1.77 us (3%)
    pallas_call x1, Pallas kernels, local(): pl.pallas_call(kernel, out_shape=jax.ShapeDtypeStruct((BR, HEADS * HD), b...  48.7 us
    unnamed x1, local copies, waits for them, and re-layouts  1.77 us

profile of v4, /device:TPU:1, one launch (start us, length us, event | category | flops | bytes accessed | tf_op | source)
XLA Modules:
  0.0 50.5 jit_solution(4527077214334006960)
XLA Ops:
  0.0 48.7 %shard_map.64 = bf16[384,512]{1,0:T(8,128)(2,1)} custom-call(s32[32]{0:T(128)} %slots.1, s32[32]{0:T(128)} %lengths.1, bf16[32,32,256]{2,1,0:T(8,128)(2,1)} %bitcast.5, bf16[192,256]{1,0:T(8,128)(2,1)} %bitcast.7, bf16[384,512]{1,0:T(8,128)(2,1)} %bitcast.6, s32[1,384]{1,0:T(1,128)} %parents_hbm.1), custom_call_target="tpu_custom_call" | custom-call | tf_op jit(solution)/shard_map/pallas_call | solution.py:333
  48.7 1.8 %copy.8 = bf16[1,384,512]{2,1,0:T(8,128)(2,1)} copy(bf16[1,384,512]{2,1,0:T(8,128)(2,1)} %bitcast.4) | data formatting | bytes 786432

commit v5 on v2

--- a/solution.py
+++ b/solution.py
@@ -18,6 +18,7 @@
 NZ = 8
 NY = 8
 CHUNKS = 4
+BLOCK = 64
 DEAD = -1e30
 SCORE_SCALE = math.log2(math.e) / math.sqrt(HD)
 
@@ -37,7 +38,7 @@
     out,
     trunk, branch, queries, parents, pick_head, pick_target,
     staged, landed, sorted_rows, keys_values, branch_staged, branch_landed, branch_kv,
-    turned, shown, top, total, summed,
+    turned, shown, top, total, summed, dead, raw, rounded,
     load, send_a, recv_a, send_b, recv_b, recv_c, send_f, recv_f, send_r, recv_r, send_p, recv_p,
 ):
     leaf = lax.axis_index("leaf")
@@ -183,28 +184,44 @@
             device_id_type=MESH,
         ).start()
 
-    def attend(keys, values, mask, first):
+    def attend(keys, values, mask_rows, first):
+        count = keys.shape[0]
         keys = jnp.concatenate([keys, keys], axis=1)
         values = jnp.transpose(values)
-        mask = jnp.concatenate([mask] * (WIDE // mask.shape[1]), axis=1)
+        blocks = [slice(at, at + BLOCK) for at in range(0, count, BLOCK)]
         for pair in range(PAIRS):
-            scores = jnp.dot(keys, turned[pair], preferred_element_type=jnp.float32) + mask
-            best = jnp.max(scores, axis=0, keepdims=True)
-            if not first:
-                best = jnp.maximum(best, top[pair])
-            weights = jnp.exp2(scores - best)
-            weight_sum = jnp.sum(weights, axis=0, keepdims=True)
+            raw[pair, :count] = jnp.dot(keys, turned[pair], preferred_element_type=jnp.float32)
+        for pair in range(PAIRS):
+            fades = []
+            for half in range(2):
+                columns = slice(half * BR, half * BR + BR)
+                best = None if first else top[pair, :, columns]
+                for block in blocks:
+                    scores = raw[pair, block, columns] + mask_rows(block)
+                    highest = jnp.max(scores, axis=0, keepdims=True)
+                    best = highest if best is None else jnp.maximum(best, highest)
+                weight_sum = None
+                for block in blocks:
+                    weights = jnp.exp2(raw[pair, block, columns] + mask_rows(block) - best)
+                    part = jnp.sum(weights, axis=0, keepdims=True)
+                    weight_sum = part if weight_sum is None else weight_sum + part
+                    rounded[pair, block, columns] = weights.astype(jnp.bfloat16)
+                if not first:
+                    fades.append(jnp.exp2(top[pair, :, columns] - best))
+                    weight_sum = total[pair, :, columns] * fades[half] + weight_sum
+                total[pair, :, columns] = weight_sum
+                top[pair, :, columns] = best
             product = jnp.dot(
-                values, weights.astype(jnp.bfloat16), preferred_element_type=jnp.float32
+                values, rounded[pair, :count], preferred_element_type=jnp.float32
             )
-            if first:
-                total[pair] = weight_sum
-                summed[pair] = product
-            else:
-                fade = jnp.exp2(top[pair] - best)
-                total[pair] = total[pair] * fade + weight_sum
-                summed[pair] = summed[pair] * fade + product
-            top[pair] = best
+            for half in range(2):
+                columns = slice(half * BR, half * BR + BR)
+                if first:
+                    summed[pair, :, columns] = product[:, columns]
+                else:
+                    summed[pair, :, columns] = (
+                        summed[pair, :, columns] * fades[half] + product[:, columns]
+                    )
 
     def attend_chunk(chunk):
         wait_bytes(keys_values.at[chunk, 1:4], recv_b.at[chunk])
@@ -218,8 +235,11 @@
         z_from = (z - dz + 8) & 7
         y_from = (y - ((key >> 2) & 7) + 8) & 7
         position = (((xh_from * 8 + z_from) * 2 + c_from) * 16 + y_from * 2 + xl_from) * 4 + (key & 3)
-        mask = jnp.where(position < lengths[slots[leaf]], 0.0, DEAD)
-        attend(both[:, :HD], both[:, HD:], mask, False)
+        dead[...] = jnp.where(position < lengths[slots[leaf]], 0.0, DEAD)
+        attend(
+            both[:, :HD], both[:, HD:],
+            lambda block: jnp.concatenate([dead[block]] * (BR // HD), axis=1), False,
+        )
 
     def attend_branch():
         wait_bytes(branch_landed.at[1], recv_p)
@@ -237,7 +257,10 @@
             ordered = moved(order, rows)
             branch_kv[0, y_from] = ordered[:48]
             branch_kv[1, y_from] = ordered[48:]
-        attend(branch_kv[0].reshape(BR, HD), branch_kv[1].reshape(BR, HD), shown[...], True)
+        attend(
+            branch_kv[0].reshape(BR, HD), branch_kv[1].reshape(BR, HD),
+            lambda block: shown[block], True,
+        )
 
     def turn_queries():
         loads[3].wait()
@@ -350,6 +373,9 @@
             pltpu.VMEM((PAIRS, 1, WIDE), f32),
             pltpu.VMEM((PAIRS, 1, WIDE), f32),
             pltpu.VMEM((PAIRS, HD, WIDE), f32),
+            pltpu.VMEM((512, HD), f32),
+            pltpu.VMEM((PAIRS, 512, WIDE), f32),
+            pltpu.VMEM((PAIRS, 512, WIDE), bf16),
             pltpu.SemaphoreType.DMA((4,)),
             pltpu.SemaphoreType.DMA,
             pltpu.SemaphoreType.DMA((CHUNKS,)),

time: 48.2 us -> 48.8 us (1.012)
  Pallas kernels: 46.3 us -> 46.8 us
    pallas_call x1, Pallas kernels: 46.3 us -> 46.8 us  [local(): pl.pallas_call(kernel, out_shape=jax.ShapeDtypeStruct((BR, HEADS * HD), b...]
where the time goes in v5:
time: 48.8 us; the launch traced here: 48.6 us
  Pallas kernels  46.8 us (96%)
  local copies, waits for them, and re-layouts  1.77 us (4%)
    pallas_call x1, Pallas kernels, local(): pl.pallas_call(kernel, out_shape=jax.ShapeDtypeStruct((BR, HEADS * HD), b...  46.8 us
    unnamed x1, local copies, waits for them, and re-layouts  1.77 us

profile of v5, /device:TPU:1, one launch (start us, length us, event | category | flops | bytes accessed | tf_op | source)
XLA Modules:
  0.0 48.6 jit_solution(9235006725484506629)
XLA Ops:
  0.0 46.8 %shard_map.64 = bf16[384,512]{1,0:T(8,128)(2,1)} custom-call(s32[32]{0:T(128)} %slots.1, s32[32]{0:T(128)} %lengths.1, bf16[32,32,256]{2,1,0:T(8,128)(2,1)} %bitcast.5, bf16[192,256]{1,0:T(8,128)(2,1)} %bitcast.7, bf16[384,512]{1,0:T(8,128)(2,1)} %bitcast.6, s32[1,384]{1,0:T(1,128)} %parents_hbm.1), custom_call_target="tpu_custom_call" | custom-call | tf_op jit(solution)/shard_map/pallas_call | solution.py:352
  46.8 1.8 %copy.8 = bf16[1,384,512]{2,1,0:T(8,128)(2,1)} copy(bf16[1,384,512]{2,1,0:T(8,128)(2,1)} %bitcast.4) | data formatting | bytes 786432

commit v6 on v5

--- a/solution.py
+++ b/solution.py
@@ -15,14 +15,23 @@
 HEADS = 4
 PAIRS = 2
 WIDE = 2 * BR
-NZ = 8
-NY = 8
 CHUNKS = 4
 BLOCK = 64
 DEAD = -1e30
 SCORE_SCALE = math.log2(math.e) / math.sqrt(HD)
 
 
+def by_distance():
+    def steps(pair):
+        return min(pair[0], 8 - pair[0]) + min(pair[1], 8 - pair[1])
+
+    pairs = sorted(((dz, dy) for dz in range(8) for dy in range(8)), key=lambda pair: (steps(pair), pair))
+    return pairs[16:32] + pairs[48:64] + pairs[32:48] + pairs[15:0:-1] + pairs[:1]
+
+
+PLANE = by_distance()
+
+
 def picks(target, rows, columns):
     row = lax.broadcasted_iota(jnp.int32, (rows, columns), 0)
     column = lax.broadcasted_iota(jnp.int32, (rows, columns), 1)
@@ -34,46 +43,48 @@
 
 
 def kernel(
-    slots, lengths, trunk_hbm, branch_hbm, queries_hbm, parents_hbm,
+    slots_hbm, lengths_hbm, trunk_hbm, branch_hbm, queries_hbm, parents_hbm,
     out,
-    trunk, branch, queries, parents, pick_head, pick_target,
+    slots, lengths, trunk, branch, queries, parents, pick_head, pick_target,
     staged, landed, sorted_rows, keys_values, branch_staged, branch_landed, branch_kv,
-    turned, shown, top, total, summed, dead, raw, rounded,
-    load, send_a, recv_a, send_b, recv_b, recv_c, send_f, recv_f, send_r, recv_r, send_p, recv_p,
+    turned, shown, top, total, summed, dead, raw, rounded, result,
+    load, send_a, recv_a, send_b, recv_b, send_r, recv_r, send_p, recv_p, store,
 ):
     leaf = lax.axis_index("leaf")
     tensor = lax.axis_index("tensor")
     xh, z, c = leaf // 16, (leaf // 2) % 8, leaf % 2
     y, xl = tensor // 2, tensor % 2
 
+    def place(xh, z, c, y, xl):
+        return ((xh * 8 + z) * 2 + c, y * 2 + xl)
+
+    def near(a, d, b):
+        return place((xh + a) % 2, z, (c + b) % 2, y, (xl + d) % 2)
+
+    barrier = pltpu.get_barrier_semaphore()
+    ring = ((1, 0, 0), (1, 0, 1), (1, 1, 0), (1, 1, 1), (0, 1, 0), (0, 1, 1), (0, 0, 1))
+
+    def signal(where):
+        pl.semaphore_signal(barrier, inc=1, device_id=where, device_id_type=MESH)
+
+    def greet(step, _):
+        signal(place(xh, (z + step // 8) % 8, c, (y + step % 8) % 8, xl))
+        return 0
+
     loads = [
-        pltpu.make_async_copy(far, near, load.at[which])
-        for which, (far, near) in enumerate(
-            [(trunk_hbm, trunk), (branch_hbm, branch), (parents_hbm, parents), (queries_hbm, queries)]
+        pltpu.make_async_copy(there, here, load.at[which])
+        for which, (there, here) in enumerate(
+            [
+                (slots_hbm, slots), (trunk_hbm, trunk), (lengths_hbm, lengths),
+                (branch_hbm, branch), (parents_hbm, parents), (queries_hbm, queries),
+            ]
         )
     ]
     for one in loads:
         one.start()
-
-    def place(xh, z, c, y, xl):
-        return ((xh * 8 + z) * 2 + c, y * 2 + xl)
-
-    def near(a, d, b):
-        return place((xh + a) % 2, z, (c + b) % 2, y, (xl + d) % 2)
-
-    barrier = pltpu.get_barrier_semaphore()
-    direct = ((1, 1, 0), (1, 1, 1), (0, 1, 0), (0, 1, 1), (0, 0, 1))
-
-    def greet(step, _):
-        pl.semaphore_signal(
-            barrier, inc=1, device_id=place(xh, (z + step // 8) % 8, c, (y + step % 8) % 8, xl),
-            device_id_type=MESH,
-        )
-        return 0
-
-    lax.fori_loop(1, NZ * NY, greet, 0)
-    for flips in direct:
-        pl.semaphore_signal(barrier, inc=1, device_id=near(*flips), device_id_type=MESH)
+    lax.fori_loop(1, 64, greet, 0)
+    for flips in ring:
+        signal(near(*flips))
 
     pick_head[...] = picks(
         lambda i: (i & 7) * 16 + (i >> 5) * 4 + ((i >> 3) & 3), 128, 128
@@ -82,51 +93,37 @@
         lambda i: ((i >> 2) & 3) * 64 + (i >> 4) * 4 + (i & 3), 256, 256
     )
 
-    def z_offset(chunk, member):
-        return (chunk + 1) % 4 if member == 0 else 7 - chunk
-
-    def stage(chunk):
-        for member in range(2):
-            z_to = (z + z_offset(chunk, member)) % 8
-            rows = jnp.concatenate(
-                [trunk[slots[((q // 2) * 8 + z_to) * 2 + q % 2]] for q in range(4)], axis=0
-            )
-            ordered = moved(pick_head[...], rows)
-            for head in range(8):
-                staged[chunk * 2 + member, head] = ordered[head * 16 : head * 16 + 16]
+    def stage(dz):
+        z_to = (z + dz) % 8
+        rows = jnp.concatenate(
+            [trunk[slots[((q // 2) * 8 + z_to) * 2 + q % 2]] for q in range(4)], axis=0
+        )
+        ordered = moved(pick_head[...], rows)
+        for head in range(8):
+            staged[dz, head] = ordered[head * 16 : head * 16 + 16]
 
     def send_plane(chunk):
-        for dy in (4, 3, 5, 2, 6, 1, 7, 0):
-            y_to = (y + dy) % 8
-            for member in range(2):
-                group = chunk * 2 + member
-                z_to = (z + z_offset(chunk, member)) % 8
-
-                def send():
-                    pltpu.make_async_remote_copy(
-                        src_ref=staged.at[group, y_to],
-                        dst_ref=landed.at[group * 8 + dy],
-                        send_sem=send_a,
-                        recv_sem=recv_a.at[chunk],
-                        device_id=place(xh, z_to, c, y_to, xl),
-                        device_id_type=MESH,
-                    ).start()
-
-                if dy == 0 and member == 0:
-                    pl.when(chunk != 3)(send)
-                else:
-                    send()
-
-    def stage_and_send(chunk, _):
-        stage(chunk)
-        send_plane(chunk)
-        return 0
+        for at in range(chunk * 16, chunk * 16 + 16):
+            dz, dy = PLANE[at]
+            if dz or dy:
+                y_to = (y + dy) % 8
+                pltpu.make_async_remote_copy(
+                    src_ref=staged.at[dz, y_to],
+                    dst_ref=landed.at[at],
+                    send_sem=send_a,
+                    recv_sem=recv_a.at[chunk],
+                    device_id=place(xh, (z + dz) % 8, c, y_to, xl),
+                    device_id_type=MESH,
+                ).start()
 
     loads[0].wait()
-    pl.semaphore_wait(barrier, NZ * NY - 1 + len(direct))
-    lax.fori_loop(0, 2, stage_and_send, 0)
-
     loads[1].wait()
+    for dz in range(8):
+        stage(dz)
+    pl.semaphore_wait(barrier, 63 + len(ring))
+    send_plane(0)
+
+    loads[3].wait()
 
     def branch_target(i):
         half = jnp.where(i >= 192, 1, 0)
@@ -153,36 +150,23 @@
         pltpu.make_async_copy(ref, ref, sem).wait()
 
     def pass_on(chunk):
-        if chunk < 3:
-            wait_bytes(landed.at[chunk * 16 : chunk * 16 + 16], recv_a.at[chunk])
-        else:
-            wait_bytes(landed.at[49:64], recv_a.at[chunk])
-        rows = landed[chunk * 16 : chunk * 16 + 16].reshape(256, 256)
+        first = chunk * 16
+        wait_bytes(landed.at[first : first + (15 if chunk == 3 else 16)], recv_a.at[chunk])
+        rows = landed[first : first + 16].reshape(256, 256)
         ordered = moved(pick_target[...], rows)
         for target in range(4):
             sorted_rows[chunk, target] = ordered[target * 64 : target * 64 + 64]
-        for a, d, b in direct:
+        for a, d, b in ring:
             target = ((xh + a) % 2) * 2 + (c + b) % 2
             pltpu.make_async_remote_copy(
                 src_ref=sorted_rows.at[chunk, target],
                 dst_ref=keys_values.at[chunk, a * 4 + d * 2 + b],
                 send_sem=send_b,
-                recv_sem=recv_c.at[chunk] if a else recv_b.at[chunk],
+                recv_sem=recv_b.at[chunk],
                 device_id=near(a, d, b),
                 device_id_type=MESH,
             ).start()
         keys_values[chunk, 0] = sorted_rows[chunk, xh * 2 + c]
-
-    def hand_on(chunk):
-        wait_bytes(keys_values.at[chunk, 6:8], recv_c.at[chunk])
-        pltpu.make_async_remote_copy(
-            src_ref=keys_values.at[chunk, 6:8],
-            dst_ref=keys_values.at[chunk, 4:6],
-            send_sem=send_f,
-            recv_sem=recv_f.at[chunk],
-            device_id=near(0, 1, 0),
-            device_id_type=MESH,
-        ).start()
 
     def attend(keys, values, mask_rows, first):
         count = keys.shape[0]
@@ -224,17 +208,21 @@
                     )
 
     def attend_chunk(chunk):
-        wait_bytes(keys_values.at[chunk, 1:4], recv_b.at[chunk])
-        wait_bytes(keys_values.at[chunk, 4:6], recv_f.at[chunk])
+        if chunk == 0:
+            loads[2].wait()
+        wait_bytes(keys_values.at[chunk, 1:8], recv_b.at[chunk])
         both = keys_values[chunk].reshape(512, 256)
-        key = lax.broadcasted_iota(jnp.int32, (512, HD), 0)
-        xh_from = (xh + (key >> 8)) & 1
-        xl_from = (xl + (key >> 7)) & 1
-        c_from = (c + (key >> 6)) & 1
-        dz = jnp.where(((key >> 5) & 1) == 0, (chunk + 1) % 4, 7 - chunk)
-        z_from = (z - dz + 8) & 7
-        y_from = (y - ((key >> 2) & 7) + 8) & 7
-        position = (((xh_from * 8 + z_from) * 2 + c_from) * 16 + y_from * 2 + xl_from) * 4 + (key & 3)
+        row = lax.broadcasted_iota(jnp.int32, (64, HD), 0)
+        inner = row & 3
+        for at in range(16):
+            dz, dy = PLANE[chunk * 16 + at]
+            start = ((z - dz + 8) % 8) * 128 + ((y - dy + 8) % 8) * 8
+            inner = inner + jnp.where((row >> 2) == at, start, 0)
+        outer = [
+            (((xh + a) % 2) * 16 + (c + b) % 2) * 64 + ((xl + d) % 2) * 4
+            for a in range(2) for d in range(2) for b in range(2)
+        ]
+        position = jnp.concatenate([inner + start for start in outer], axis=0)
         dead[...] = jnp.where(position < lengths[slots[leaf]], 0.0, DEAD)
         attend(
             both[:, :HD], both[:, HD:],
@@ -263,7 +251,7 @@
         )
 
     def turn_queries():
-        loads[3].wait()
+        loads[5].wait()
         for head in range(HEADS):
             flipped = jnp.transpose(queries[:, head * HD : head * HD + HD])
             scaled = flipped.astype(jnp.float32) * SCORE_SCALE
@@ -274,7 +262,7 @@
             turned[head // 2, HD:, columns] = fine
 
     def mark_ancestors():
-        loads[2].wait()
+        loads[4].wait()
         above = lax.broadcasted_iota(jnp.int32, (HD, HD), 0)
         along = lax.broadcasted_iota(jnp.int32, (HD, HD), 1)
 
@@ -305,56 +293,62 @@
                     mask = jnp.full((HD, HD), DEAD, jnp.float32)
                 shown[up * HD : up * HD + HD, down * HD : down * HD + HD] = mask
 
-    lax.fori_loop(2, 3, stage_and_send, 0)
+    def hand_branch():
+        wait_bytes(branch_landed.at[0, 1:8], recv_r)
+        pltpu.make_async_remote_copy(
+            src_ref=branch_landed.at[0],
+            dst_ref=branch_landed.at[1],
+            send_sem=send_p,
+            recv_sem=recv_p,
+            device_id=near(0, 1, 0),
+            device_id_type=MESH,
+        ).start()
+
+    send_plane(1)
+    send_plane(2)
     pass_on(0)
-    lax.fori_loop(3, 4, stage_and_send, 0)
-    landed[48] = staged[6, y]
+    send_plane(3)
+    landed[63] = staged[0, y]
+    turn_queries()
     pass_on(1)
-    hand_on(0)
-    turn_queries()
-    wait_bytes(branch_landed.at[0, 1:8], recv_r)
-    pltpu.make_async_remote_copy(
-        src_ref=branch_landed.at[0],
-        dst_ref=branch_landed.at[1],
-        send_sem=send_p,
-        recv_sem=recv_p,
-        device_id=near(0, 1, 0),
-        device_id_type=MESH,
-    ).start()
+    hand_branch()
     mark_ancestors()
     pass_on(2)
-    hand_on(1)
     attend_branch()
     pass_on(3)
-    hand_on(2)
     attend_chunk(0)
-    hand_on(3)
     attend_chunk(1)
     attend_chunk(2)
     attend_chunk(3)
 
+    stores = []
     for head in range(HEADS):
         columns = slice((head % 2) * BR, (head % 2) * BR + BR)
-        result = summed[head // 2, :, columns] * (1.0 / total[head // 2, :, columns])
-        out[:, head * HD : head * HD + HD] = jnp.transpose(result.astype(jnp.bfloat16))
-
-    wait_bytes(landed.at[1:64], send_a)
+        lanes = slice(head * HD, head * HD + HD)
+        normal = summed[head // 2, :, columns] * (1.0 / total[head // 2, :, columns])
+        result[:, lanes] = jnp.transpose(normal.astype(jnp.bfloat16))
+        stores.append(pltpu.make_async_copy(result.at[:, lanes], out.at[:, lanes], store.at[head]))
+        stores[-1].start()
+    for one in stores:
+        one.wait()
+
+    wait_bytes(landed.at[0:63], send_a)
     wait_bytes(branch_landed.at[0, 1:8], send_r)
     wait_bytes(branch_landed.at[0], send_p)
-    wait_bytes(keys_values.at[:, 0:5], send_b)
-    wait_bytes(keys_values.at[:, 0:2], send_f)
+    wait_bytes(keys_values.at[:, 1:8], send_b)
 
 
 def local(trunk_kv, slot_trees, trunk_len, parents, queries, branch_kv):
-    smem = pl.BlockSpec(memory_space=pltpu.SMEM)
     hbm = pl.BlockSpec(memory_space=pltpu.HBM)
     bf16, f32 = jnp.bfloat16, jnp.float32
     attended = pl.pallas_call(
         kernel,
         out_shape=jax.ShapeDtypeStruct((BR, HEADS * HD), bf16),
-        in_specs=[smem, smem, hbm, hbm, hbm, hbm],
-        out_specs=pl.BlockSpec(memory_space=pltpu.VMEM),
+        in_specs=[hbm] * 6,
+        out_specs=hbm,
         scratch_shapes=[
+            pltpu.SMEM((TREES,), jnp.int32),
+            pltpu.SMEM((TREES,), jnp.int32),
             pltpu.VMEM((TREES, 32, 256), bf16),
             pltpu.VMEM((192, 256), bf16),
             pltpu.VMEM((BR, HEADS * HD), bf16),
@@ -376,18 +370,17 @@
             pltpu.VMEM((512, HD), f32),
             pltpu.VMEM((PAIRS, 512, WIDE), f32),
             pltpu.VMEM((PAIRS, 512, WIDE), bf16),
-            pltpu.SemaphoreType.DMA((4,)),
+            pltpu.VMEM((BR, HEADS * HD), bf16),
+            pltpu.SemaphoreType.DMA((6,)),
             pltpu.SemaphoreType.DMA,
             pltpu.SemaphoreType.DMA((CHUNKS,)),
             pltpu.SemaphoreType.DMA,
             pltpu.SemaphoreType.DMA((CHUNKS,)),
-            pltpu.SemaphoreType.DMA((CHUNKS,)),
-            pltpu.SemaphoreType.DMA,
-            pltpu.SemaphoreType.DMA((CHUNKS,)),
-            pltpu.SemaphoreType.DMA,
-            pltpu.SemaphoreType.DMA,
-            pltpu.SemaphoreType.DMA,
-            pltpu.SemaphoreType.DMA,
+            pltpu.SemaphoreType.DMA,
+            pltpu.SemaphoreType.DMA,
+            pltpu.SemaphoreType.DMA,
+            pltpu.SemaphoreType.DMA,
+            pltpu.SemaphoreType.DMA((HEADS,)),
         ],
         compiler_params=pltpu.CompilerParams(
             collective_id=0, has_side_effects=True, vmem_limit_bytes=60 * 1024 * 1024

time: 48.8 us -> 49.2 us (level)
  no operation moved by 1% of the time
where the time goes in v6:
time: 49.2 us; the launch traced here: 48.8 us
  Pallas kernels  47 us (96%)
  local copies, waits for them, and re-layouts  1.77 us (4%)
    pallas_call x1, Pallas kernels, local(): pl.pallas_call(kernel, out_shape=jax.ShapeDtypeStruct((BR, HEADS * HD), b...  47 us
    unnamed x1, local copies, waits for them, and re-layouts  1.77 us

profile of v6, /device:TPU:1, one launch (start us, length us, event | category | flops | bytes accessed | tf_op | source)
XLA Modules:
  0.0 48.8 jit_solution(15299920129252371228)
XLA Ops:
  0.0 47.0 %shard_map.64 = bf16[384,512]{1,0:T(8,128)(2,1)} custom-call(s32[32]{0:T(128)} %slots_hbm.1, s32[32]{0:T(128)} %lengths_hbm.1, bf16[32,32,256]{2,1,0:T(8,128)(2,1)} %bitcast.5, bf16[192,256]{1,0:T(8,128)(2,1)} %bitcast.7, bf16[384,512]{1,0:T(8,128)(2,1)} %bitcast.6, s32[1,384]{1,0:T(1,128)} %parents_hbm.1), custom_call_target="tpu_custom_call" | custom-call | tf_op jit(solution)/shard_map/pallas_call | solution.py:344
  47.0 1.8 %copy.8 = bf16[1,384,512]{2,1,0:T(8,128)(2,1)} copy(bf16[1,384,512]{2,1,0:T(8,128)(2,1)} %bitcast.4) | data formatting | bytes 786432

commit v7 on v6

--- a/solution.py
+++ b/solution.py
@@ -25,8 +25,10 @@
     def steps(pair):
         return min(pair[0], 8 - pair[0]) + min(pair[1], 8 - pair[1])
 
-    pairs = sorted(((dz, dy) for dz in range(8) for dy in range(8)), key=lambda pair: (steps(pair), pair))
-    return pairs[16:32] + pairs[48:64] + pairs[32:48] + pairs[15:0:-1] + pairs[:1]
+    ways = (4, 3, 5, 2, 6, 1, 7)
+    first = [(0, dy) for dy in ways] + [(dz, 0) for dz in ways]
+    others = sorted(((dz, dy) for dz in ways for dy in ways), key=lambda pair: -steps(pair))
+    return first + others + [(0, 0)]
 
 
 PLANE = by_distance()
@@ -48,7 +50,7 @@
     slots, lengths, trunk, branch, queries, parents, pick_head, pick_target,
     staged, landed, sorted_rows, keys_values, branch_staged, branch_landed, branch_kv,
     turned, shown, top, total, summed, dead, raw, rounded, result,
-    load, send_a, recv_a, send_b, recv_b, send_r, recv_r, send_p, recv_p, store,
+    load, send_a, recv_a, send_b, recv_b, send_r, recv_r, send_p, recv_p, store, rows_in,
 ):
     leaf = lax.axis_index("leaf")
     tensor = lax.axis_index("tensor")
@@ -67,9 +69,11 @@
     def signal(where):
         pl.semaphore_signal(barrier, inc=1, device_id=where, device_id_type=MESH)
 
-    def greet(step, _):
-        signal(place(xh, (z + step // 8) % 8, c, (y + step % 8) % 8, xl))
-        return 0
+    for step in range(1, 8):
+        signal(place(xh, z, c, (y + step) % 8, xl))
+        signal(place(xh, (z + step) % 8, c, y, xl))
+    for flips in ring:
+        signal(near(*flips))
 
     loads = [
         pltpu.make_async_copy(there, here, load.at[which])
@@ -82,10 +86,6 @@
     ]
     for one in loads:
         one.start()
-    lax.fori_loop(1, 64, greet, 0)
-    for flips in ring:
-        signal(near(*flips))
-
     pick_head[...] = picks(
         lambda i: (i & 7) * 16 + (i >> 5) * 4 + ((i >> 3) & 3), 128, 128
     )
@@ -102,8 +102,8 @@
         for head in range(8):
             staged[dz, head] = ordered[head * 16 : head * 16 + 16]
 
-    def send_plane(chunk):
-        for at in range(chunk * 16, chunk * 16 + 16):
+    def send_plane(first, end):
+        for at in range(first, end):
             dz, dy = PLANE[at]
             if dz or dy:
                 y_to = (y + dy) % 8
@@ -111,17 +111,25 @@
                     src_ref=staged.at[dz, y_to],
                     dst_ref=landed.at[at],
                     send_sem=send_a,
-                    recv_sem=recv_a.at[chunk],
+                    recv_sem=recv_a.at[at // 16],
                     device_id=place(xh, (z + dz) % 8, c, y_to, xl),
                     device_id_type=MESH,
                 ).start()
 
     loads[0].wait()
     loads[1].wait()
-    for dz in range(8):
-        stage(dz)
-    pl.semaphore_wait(barrier, 63 + len(ring))
-    send_plane(0)
+    stage(0)
+    pl.semaphore_wait(barrier, 14 + len(ring))
+    for step in range(1, 8):
+        pl.semaphore_signal(
+            rows_in, inc=1, device_id=place(xh, (z + step) % 8, c, y, xl), device_id_type=MESH
+        )
+    send_plane(0, 7)
+    for at in range(7, 14):
+        stage(PLANE[at][0])
+        send_plane(at, at + 1)
+    pl.semaphore_wait(rows_in, 7)
+    send_plane(14, 16)
 
     loads[3].wait()
 
@@ -304,10 +312,9 @@
             device_id_type=MESH,
         ).start()
 
-    send_plane(1)
-    send_plane(2)
+    send_plane(16, 48)
     pass_on(0)
-    send_plane(3)
+    send_plane(48, 64)
     landed[63] = staged[0, y]
     turn_queries()
     pass_on(1)
@@ -381,6 +388,7 @@
             pltpu.SemaphoreType.DMA,
             pltpu.SemaphoreType.DMA,
             pltpu.SemaphoreType.DMA((HEADS,)),
+            pltpu.SemaphoreType.REGULAR,
         ],
         compiler_params=pltpu.CompilerParams(
             collective_id=0, has_side_effects=True, vmem_limit_bytes=60 * 1024 * 1024

time: 49.2 us -> 48.3 us (0.982)
  Pallas kernels: 47 us -> 46.3 us
    pallas_call x1, Pallas kernels: 47 us -> 46.3 us  [local(): pl.pallas_call(kernel, out_shape=jax.ShapeDtypeStruct((BR, HEADS * HD), b...]
where the time goes in v7:
time: 48.3 us; the launch traced here: 48.1 us
  Pallas kernels  46.3 us (96%)
  local copies, waits for them, and re-layouts  1.77 us (4%)
    pallas_call x1, Pallas kernels, local(): pl.pallas_call(kernel, out_shape=jax.ShapeDtypeStruct((BR, HEADS * HD), b...  46.3 us
    unnamed x1, local copies, waits for them, and re-layouts  1.77 us

profile of v7, /device:TPU:1, one launch (start us, length us, event | category | flops | bytes accessed | tf_op | source)
XLA Modules:
  0.0 48.1 jit_solution(14688019202041550567)
XLA Ops:
  0.0 46.3 %shard_map.64 = bf16[384,512]{1,0:T(8,128)(2,1)} custom-call(s32[32]{0:T(128)} %slots_hbm.1, s32[32]{0:T(128)} %lengths_hbm.1, bf16[32,32,256]{2,1,0:T(8,128)(2,1)} %bitcast.5, bf16[192,256]{1,0:T(8,128)(2,1)} %bitcast.7, bf16[384,512]{1,0:T(8,128)(2,1)} %bitcast.6, s32[1,384]{1,0:T(1,128)} %parents_hbm.1), custom_call_target="tpu_custom_call" | custom-call | tf_op jit(solution)/shard_map/pallas_call | solution.py:351
  46.4 1.8 %copy.8 = bf16[1,384,512]{2,1,0:T(8,128)(2,1)} copy(bf16[1,384,512]{2,1,0:T(8,128)(2,1)} %bitcast.4) | data formatting | bytes 786432

commit v8 on v7

--- a/solution.py
+++ b/solution.py
@@ -15,7 +15,9 @@
 HEADS = 4
 PAIRS = 2
 WIDE = 2 * BR
-CHUNKS = 4
+BOUNDS = (0, 16, 40, 56, 64)
+CHUNKS = len(BOUNDS) - 1
+WIDEST = 24 * 32
 BLOCK = 64
 DEAD = -1e30
 SCORE_SCALE = math.log2(math.e) / math.sqrt(HD)
@@ -90,7 +92,7 @@
         lambda i: (i & 7) * 16 + (i >> 5) * 4 + ((i >> 3) & 3), 128, 128
     )
     pick_target[...] = picks(
-        lambda i: ((i >> 2) & 3) * 64 + (i >> 4) * 4 + (i & 3), 256, 256
+        lambda i: ((i >> 2) & 3) * 32 + (i >> 4) * 4 + (i & 3), 128, 128
     )
 
     def stage(dz):
@@ -111,7 +113,7 @@
                     src_ref=staged.at[dz, y_to],
                     dst_ref=landed.at[at],
                     send_sem=send_a,
-                    recv_sem=recv_a.at[at // 16],
+                    recv_sem=recv_a.at[sum(at >= bound for bound in BOUNDS[1:])],
                     device_id=place(xh, (z + dz) % 8, c, y_to, xl),
                     device_id_type=MESH,
                 ).start()
@@ -158,23 +160,24 @@
         pltpu.make_async_copy(ref, ref, sem).wait()
 
     def pass_on(chunk):
-        first = chunk * 16
-        wait_bytes(landed.at[first : first + (15 if chunk == 3 else 16)], recv_a.at[chunk])
-        rows = landed[first : first + 16].reshape(256, 256)
-        ordered = moved(pick_target[...], rows)
-        for target in range(4):
-            sorted_rows[chunk, target] = ordered[target * 64 : target * 64 + 64]
+        first, end = BOUNDS[chunk], BOUNDS[chunk + 1]
+        wait_bytes(landed.at[first : end - 1 if chunk == CHUNKS - 1 else end], recv_a.at[chunk])
+        for at in range(first, end, 8):
+            ordered = moved(pick_target[...], landed[at : at + 8].reshape(128, 256))
+            for target in range(4):
+                sorted_rows[target, at * 4 : at * 4 + 32] = ordered[target * 32 : target * 32 + 32]
+        rows = slice(first * 4, end * 4)
         for a, d, b in ring:
             target = ((xh + a) % 2) * 2 + (c + b) % 2
             pltpu.make_async_remote_copy(
-                src_ref=sorted_rows.at[chunk, target],
-                dst_ref=keys_values.at[chunk, a * 4 + d * 2 + b],
+                src_ref=sorted_rows.at[target, rows],
+                dst_ref=keys_values.at[a * 4 + d * 2 + b, rows],
                 send_sem=send_b,
                 recv_sem=recv_b.at[chunk],
                 device_id=near(a, d, b),
                 device_id_type=MESH,
             ).start()
-        keys_values[chunk, 0] = sorted_rows[chunk, xh * 2 + c]
+        keys_values[0, rows] = sorted_rows[xh * 2 + c, rows]
 
     def attend(keys, values, mask_rows, first):
         count = keys.shape[0]
@@ -218,20 +221,22 @@
     def attend_chunk(chunk):
         if chunk == 0:
             loads[2].wait()
-        wait_bytes(keys_values.at[chunk, 1:8], recv_b.at[chunk])
-        both = keys_values[chunk].reshape(512, 256)
-        row = lax.broadcasted_iota(jnp.int32, (64, HD), 0)
+        first, end = BOUNDS[chunk], BOUNDS[chunk + 1]
+        count = (end - first) * 32
+        wait_bytes(keys_values.at[1:8, first * 4 : end * 4], recv_b.at[chunk])
+        both = keys_values[:, first * 4 : end * 4].reshape(count, 256)
+        row = lax.broadcasted_iota(jnp.int32, (count // 8, HD), 0)
         inner = row & 3
-        for at in range(16):
-            dz, dy = PLANE[chunk * 16 + at]
+        for at in range(first, end):
+            dz, dy = PLANE[at]
             start = ((z - dz + 8) % 8) * 128 + ((y - dy + 8) % 8) * 8
-            inner = inner + jnp.where((row >> 2) == at, start, 0)
+            inner = inner + jnp.where((row >> 2) == at - first, start, 0)
         outer = [
             (((xh + a) % 2) * 16 + (c + b) % 2) * 64 + ((xl + d) % 2) * 4
             for a in range(2) for d in range(2) for b in range(2)
         ]
         position = jnp.concatenate([inner + start for start in outer], axis=0)
-        dead[...] = jnp.where(position < lengths[slots[leaf]], 0.0, DEAD)
+        dead[:count] = jnp.where(position < lengths[slots[leaf]], 0.0, DEAD)
         attend(
             both[:, :HD], both[:, HD:],
             lambda block: jnp.concatenate([dead[block]] * (BR // HD), axis=1), False,
@@ -342,7 +347,7 @@
     wait_bytes(landed.at[0:63], send_a)
     wait_bytes(branch_landed.at[0, 1:8], send_r)
     wait_bytes(branch_landed.at[0], send_p)
-    wait_bytes(keys_values.at[:, 1:8], send_b)
+    wait_bytes(keys_values.at[1:8], send_b)
 
 
 def local(trunk_kv, slot_trees, trunk_len, parents, queries, branch_kv):
@@ -361,11 +366,11 @@
             pltpu.VMEM((BR, HEADS * HD), bf16),
             pltpu.VMEM((1, BR), jnp.int32),
             pltpu.VMEM((128, 128), bf16),
-            pltpu.VMEM((256, 256), bf16),
+            pltpu.VMEM((128, 128), bf16),
             pltpu.VMEM((8, 8, 16, 256), bf16),
             pltpu.VMEM((64, 16, 256), bf16),
-            pltpu.VMEM((CHUNKS, 4, 64, 256), bf16),
-            pltpu.VMEM((CHUNKS, 8, 64, 256), bf16),
+            pltpu.VMEM((4, 256, 256), bf16),
+            pltpu.VMEM((8, 256, 256), bf16),
             pltpu.VMEM((8, 48, HD), bf16),
             pltpu.VMEM((2, 8, 48, HD), bf16),
             pltpu.VMEM((2, 8, 48, HD), bf16),
@@ -374,9 +379,9 @@
             pltpu.VMEM((PAIRS, 1, WIDE), f32),
             pltpu.VMEM((PAIRS, 1, WIDE), f32),
             pltpu.VMEM((PAIRS, HD, WIDE), f32),
-            pltpu.VMEM((512, HD), f32),
-            pltpu.VMEM((PAIRS, 512, WIDE), f32),
-            pltpu.VMEM((PAIRS, 512, WIDE), bf16),
+            pltpu.VMEM((WIDEST, HD), f32),
+            pltpu.VMEM((PAIRS, WIDEST, WIDE), f32),
+            pltpu.VMEM((PAIRS, WIDEST, WIDE), bf16),
             pltpu.VMEM((BR, HEADS * HD), bf16),
             pltpu.SemaphoreType.DMA((6,)),
             pltpu.SemaphoreType.DMA,

time: 48.3 us -> 49.1 us (1.017)
  Pallas kernels: 46.3 us -> 47 us
    pallas_call x1, Pallas kernels: 46.3 us -> 47 us  [local(): pl.pallas_call(kernel, out_shape=jax.ShapeDtypeStruct((BR, HEADS * HD), b...]
where the time goes in v8:
time: 49.1 us; the launch traced here: 48.8 us
  Pallas kernels  47 us (96%)
  local copies, waits for them, and re-layouts  1.77 us (4%)
    pallas_call x1, Pallas kernels, local(): pl.pallas_call(kernel, out_shape=jax.ShapeDtypeStruct((BR, HEADS * HD), b...  47 us
    unnamed x1, local copies, waits for them, and re-layouts  1.77 us

profile of v8, /device:TPU:1, one launch (start us, length us, event | category | flops | bytes accessed | tf_op | source)
XLA Modules:
  0.0 48.8 jit_solution(9736423014102728105)
XLA Ops:
  0.0 47.0 %shard_map.64 = bf16[384,512]{1,0:T(8,128)(2,1)} custom-call(s32[32]{0:T(128)} %slots_hbm.1, s32[32]{0:T(128)} %lengths_hbm.1, bf16[32,32,256]{2,1,0:T(8,128)(2,1)} %bitcast.5, bf16[192,256]{1,0:T(8,128)(2,1)} %bitcast.7, bf16[384,512]{1,0:T(8,128)(2,1)} %bitcast.6, s32[1,384]{1,0:T(1,128)} %parents_hbm.1), custom_call_target="tpu_custom_call" | custom-call | tf_op jit(solution)/shard_map/pallas_call | solution.py:356
  47.1 1.8 %copy.8 = bf16[1,384,512]{2,1,0:T(8,128)(2,1)} copy(bf16[1,384,512]{2,1,0:T(8,128)(2,1)} %bitcast.4) | data formatting | bytes 786432

commit v9 on v7

--- a/solution.py
+++ b/solution.py
@@ -321,8 +321,8 @@
     hand_branch()
     mark_ancestors()
     pass_on(2)
+    pass_on(3)
     attend_branch()
-    pass_on(3)
     attend_chunk(0)
     attend_chunk(1)
     attend_chunk(2)

time: 48.3 us -> 46.6 us (0.965)
  the two profiles are of different devices: /device:TPU:1 before, /device:TPU:4 now
where the time goes in v9:
time: 46.6 us; the launch traced here: 46.4 us
  Pallas kernels  44.7 us (96%)
  local copies, waits for them, and re-layouts  1.77 us (4%)
    pallas_call x1, Pallas kernels, local(): pl.pallas_call(kernel, out_shape=jax.ShapeDtypeStruct((BR, HEADS * HD), b...  44.7 us
    unnamed x1, local copies, waits for them, and re-layouts  1.77 us

profile of v9, /device:TPU:4, one launch (start us, length us, event | category | flops | bytes accessed | tf_op | source)
XLA Modules:
  0.0 46.4 jit_solution(4442865809200709875)
XLA Ops:
  0.0 44.7 %shard_map.64 = bf16[384,512]{1,0:T(8,128)(2,1)} custom-call(s32[32]{0:T(128)} %slots_hbm.1, s32[32]{0:T(128)} %lengths_hbm.1, bf16[32,32,256]{2,1,0:T(8,128)(2,1)} %bitcast.5, bf16[192,256]{1,0:T(8,128)(2,1)} %bitcast.7, bf16[384,512]{1,0:T(8,128)(2,1)} %bitcast.6, s32[1,384]{1,0:T(1,128)} %parents_hbm.1), custom_call_target="tpu_custom_call" | custom-call | tf_op jit(solution)/shard_map/pallas_call | solution.py:351
  44.7 1.8 %copy.8 = bf16[1,384,512]{2,1,0:T(8,128)(2,1)} copy(bf16[1,384,512]{2,1,0:T(8,128)(2,1)} %bitcast.4) | data formatting | bytes 786432

commit v10 on v9

--- a/solution.py
+++ b/solution.py
@@ -319,9 +319,9 @@
     turn_queries()
     pass_on(1)
     hand_branch()
-    mark_ancestors()
     pass_on(2)
     pass_on(3)
+    mark_ancestors()
     attend_branch()
     attend_chunk(0)
     attend_chunk(1)

time: 46.6 us -> 46.6 us (level)
  no operation moved by 1% of the time
where the time goes in v10:
time: 46.6 us; the launch traced here: 46.5 us
  Pallas kernels  44.7 us (96%)
  local copies, waits for them, and re-layouts  1.77 us (4%)
    pallas_call x1, Pallas kernels, local(): pl.pallas_call(kernel, out_shape=jax.ShapeDtypeStruct((BR, HEADS * HD), b...  44.7 us
    unnamed x1, local copies, waits for them, and re-layouts  1.77 us

profile of v10, /device:TPU:4, one launch (start us, length us, event | category | flops | bytes accessed | tf_op | source)
XLA Modules:
  0.0 46.5 jit_solution(9125318929595731575)
XLA Ops:
  0.0 44.7 %shard_map.64 = bf16[384,512]{1,0:T(8,128)(2,1)} custom-call(s32[32]{0:T(128)} %slots_hbm.1, s32[32]{0:T(128)} %lengths_hbm.1, bf16[32,32,256]{2,1,0:T(8,128)(2,1)} %bitcast.5, bf16[192,256]{1,0:T(8,128)(2,1)} %bitcast.7, bf16[384,512]{1,0:T(8,128)(2,1)} %bitcast.6, s32[1,384]{1,0:T(1,128)} %parents_hbm.1), custom_call_target="tpu_custom_call" | custom-call | tf_op jit(solution)/shard_map/pallas_call | solution.py:351
  44.7 1.8 %copy.8 = bf16[1,384,512]{2,1,0:T(8,128)(2,1)} copy(bf16[1,384,512]{2,1,0:T(8,128)(2,1)} %bitcast.4) | data formatting | bytes 786432
